TPU v7x, 32 devices: a whole 2x2x4 slice. The times are simulated.
32 devices in a mesh: groups: 2 (over y), dp: 8 (over z, x), mp: 2 (over core).
Axes of the slice: x: 2, y: 2, z: 4, core: 2. Of those that a mesh axis runs over, the one named last changes fastest.
Arguments:
- acts: bfloat16 [2048, 4096], P(('groups', 'dp'), 'mp'), parts along dimension 0, may hold values from -45 to 45
- out_grads: bfloat16 [2048, 11008], P(('groups', 'dp'), 'mp'), parts along dimension 0, may hold values from -6 to 6
- in_proj: bfloat16 [4096, 32], P('mp'), may hold values from -0.09375 to 0.09375
- out_proj: bfloat16 [11008, 32], P('mp'), may hold values from -0.0546875 to 0.0546875
- example_ids: int32 [16, 128], P(('groups', 'dp')), parts along dimension 0, may hold values from 0 to 7, never falling along the last dimension, each value on 1 to 64 neighbouring positions
- query_ids: int32 [2048], P(('groups', 'mp')), parts along dimension 0, may hold values from 0 to 63
Outputs:
- scores: float32 [2048, 64], P(('groups', 'mp'), 'dp'), parts along dimension 0
There are 2 independent parts, one for each index of `groups`. A program takes and returns all parts, laid end to end along the dimension named above; an argument that names none is the same for every part. Nothing has to cross between parts.
Inputs may be any that keep to these rules, and one draw needn't show every extreme that they name: `example_ids`: along each row the example numbers never fall; each of the 8 examples of a row has 1 to 64 tokens.
All inputs are finite; a program needn't handle non-finite values.
Results may differ from a plain program's by a relative error of at most 0.0003.
Values may be sent and summed in bfloat16 or wider, within the bound.
No kernel may reach another device: no remote copies, remote signals or barrier semaphores. Data moves between devices by JAX's collectives and lax.ppermute only.
A program may use at most 64 MiB of HBM per device.

v0:
```python
import jax
import jax.numpy as jnp
from jax import lax
from jax.sharding import PartitionSpec as P

E_DEV = 8


def chol_solve(factor, rhs):
    inner = lax.linalg.triangular_solve(factor, rhs, left_side=True, lower=True)
    return lax.linalg.triangular_solve(factor, inner, left_side=True, lower=True, transpose_a=True)


def local(acts, out_grads, in_proj, out_proj, example_ids, query_ids):
    part_in = jnp.dot(acts, in_proj, preferred_element_type=jnp.float32)
    part_out = jnp.dot(out_grads, out_proj, preferred_element_type=jnp.float32)
    full_in, full_out = lax.psum((part_in, part_out), "mp")
    left = full_in.astype(jnp.bfloat16)
    right = full_out.astype(jnp.bfloat16)
    tok_count = left.shape[0]
    rin_size = left.shape[1]
    rout_size = right.shape[1]
    ex_count = E_DEV
    k_size = rin_size * rout_size
    ids = example_ids[0]
    onehot = (ids[:, None] == jnp.arange(ex_count, dtype=jnp.int32)[None, :]).astype(jnp.bfloat16)
    wide = (onehot[:, :, None] * left[:, None, :]).reshape(tok_count, ex_count * rin_size)
    summed = lax.dot_general(
        right, wide, (((0,), (0,)), ((), ())), preferred_element_type=jnp.float32
    )
    local_sk = (
        summed.reshape(rout_size, ex_count, rin_size)
        .transpose(1, 0, 2)
        .reshape(ex_count, k_size)
        .astype(jnp.bfloat16)
    )
    every_sk = lax.all_gather(local_sk, "dp", axis=0, tiled=True)
    gram = lax.dot_general(
        every_sk, every_sk, (((0,), (0,)), ((), ())), preferred_element_type=jnp.float32
    )
    local_f32 = local_sk.astype(jnp.float32)
    total_sq = lax.psum(jnp.sum(local_f32 * local_f32), "dp")
    damping = 0.1 * total_sq / k_size
    damped = gram + damping * jnp.eye(k_size, dtype=jnp.float32)
    factor = jnp.linalg.cholesky(damped)
    queried = jnp.take(every_sk, query_ids, axis=0).astype(jnp.float32)
    precond = chol_solve(factor, queried.T)
    return lax.dot_general(
        precond, local_f32, (((0,), (1,)), ((), ())), precision=lax.Precision.HIGHEST
    )


def solution(mesh):
    in_specs = (
        P(("groups", "dp"), "mp"),
        P(("groups", "dp"), "mp"),
        P("mp", None),
        P("mp", None),
        P(("groups", "dp"), None),
        P(("groups", "mp")),
    )
    out_specs = P(("groups", "mp"), "dp")
    return jax.shard_map(local, mesh=mesh, in_specs=in_specs, out_specs=out_specs, check_vma=False)
```

profile of v0, /device:TPU:0, one launch (start us, length us, event | category | flops | bytes accessed | tf_op | source)
XLA Modules:
  0.0 430.1 jit_solution(15327840756639629045)
XLA Ops:
  2.2 1.3 fusion.105
  3.5 1.5 fusion.104
  5.0 3.7 all-reduce.1
  9.6 23.4 %psum.23 = f32[]{:T(128)} all-reduce(f32[]{:T(128)} %get-tuple-element.66), channel_id=1, replica_groups=mesh['groups'=2,'dp'=8,'mp'=2] {'dp'}, use_global_device_ids=true, to_apply=%region_3.0 | all-reduce | flops 1 | bytes 8 | tf_op jit(solution)/shard_map/psum | solution.py:42
  33.8 30.5 %all_gather.3 = bf16[64,1024]{1,0:T(8,128)(2,1)S(1)} all-gather(bf16[8,1024]{1,0:T(8,128)(2,1)S(1)} %convert_element_type.39), channel_id=1, replica_groups=mesh['groups'=2,'dp'=8,'mp'=2] {'dp'}, dimensions={0}, use_global_device_ids=true | all-gather | bytes 147456 | tf_op jit(solution)/shard_map/all_gather | solution.py:37
  64.3 2.1 gather_fusion
  66.4 2.1 fusion.102
  68.4 2.7 fusion.106
  71.1 5.8 %copy.7 = f32[1024,1024]{0,1:T(8,128)} copy(f32[1024,1024]{1,0:T(8,128)} %fusion.106) | data formatting | bytes 8388608 | tf_op jit(solution)/shard_map/dot_general | solution.py:38
  76.9 4.4 %fusion.1 = f32[1024,1024]{1,0:T(8,128)S(1)} fusion(f32[1024,1024]{0,1:T(8,128)} %copy.7, f32[1024,1024]{1,0:T(8,128)} %fusion.106, f32[]{:T(128)S(6)} %div.11), kind=kLoop, calls=%fused_computation.6 | loop fusion | flops 8388608 | bytes 12582916 | tf_op jit(solution)/shard_map/jit(cholesky)/div | solution.py:45
  81.3 1.9 copy-done.2
  83.3 11.7 %cholesky.222 = f32[128,128]{1,0:T(8,128)S(1)} custom-call(f32[128,128]{1,0:T(8,128)S(1)} %cholesky.577), custom_call_target="Cholesky" | custom-call | tf_op jit(solution)/shard_map/jit(cholesky)/cholesky | solution.py:45
  95.0 9.8 %custom-call.64 = f32[1,128,128]{1,2,0:T(8,128)S(1)} custom-call(f32[1,128,128]{2,1,0:T(8,128)S(1)} %get-tuple-element.65), custom_call_target="InvertDiagBlocksLowerTriangular" | custom-call | tf_op jit(solution)/shard_map/jit(cholesky)/cholesky | solution.py:45
  104.8 2.5 cholesky.254
  107.3 2.4 constant_dynamic-update-slice_fusion.50
  109.7 1.5 convolution_subtract_fusion
  111.3 11.9 %cholesky.243 = f32[128,128]{1,0:T(8,128)S(1)} custom-call(f32[128,128]{1,0:T(8,128)S(1)} %cholesky.581), custom_call_target="Cholesky" | custom-call | tf_op jit(solution)/shard_map/jit(cholesky)/cholesky | solution.py:45
  125.8 9.8 %custom-call.65 = f32[1,128,128]{1,2,0:T(8,128)S(1)} custom-call(f32[1,128,128]{2,1,0:T(8,128)S(1)} %get-tuple-element.62), custom_call_target="InvertDiagBlocksLowerTriangular" | custom-call | tf_op jit(solution)/shard_map/jit(cholesky)/cholesky | solution.py:45
  135.6 1.2 convolution_dynamic-update-slice_fusion
  136.8 2.1 convolution_subtract_fusion.1
  138.9 11.7 %cholesky.466 = f32[128,128]{1,0:T(8,128)S(1)} custom-call(f32[128,128]{1,0:T(8,128)S(1)} %cholesky.586), custom_call_target="Cholesky" | custom-call | tf_op jit(solution)/shard_map/jit(cholesky)/cholesky | solution.py:45
  152.6 9.8 %custom-call.66 = f32[1,128,128]{1,2,0:T(8,128)S(1)} custom-call(f32[1,128,128]{2,1,0:T(8,128)S(1)} %get-tuple-element.59), custom_call_target="InvertDiagBlocksLowerTriangular" | custom-call | tf_op jit(solution)/shard_map/jit(cholesky)/cholesky | solution.py:45
  162.4 1.2 convolution_dynamic-update-slice_fusion.1
  163.5 2.3 convolution_subtract_fusion.2
  165.9 11.9 %cholesky.485 = f32[128,128]{1,0:T(8,128)S(1)} custom-call(f32[128,128]{1,0:T(8,128)S(1)} %cholesky.591), custom_call_target="Cholesky" | custom-call | tf_op jit(solution)/shard_map/jit(cholesky)/cholesky | solution.py:45
  179.8 9.8 %custom-call.67 = f32[1,128,128]{1,2,0:T(8,128)S(1)} custom-call(f32[1,128,128]{2,1,0:T(8,128)S(1)} %get-tuple-element.56), custom_call_target="InvertDiagBlocksLowerTriangular" | custom-call | tf_op jit(solution)/shard_map/jit(cholesky)/cholesky | solution.py:45
  189.6 1.1 convolution_dynamic-update-slice_fusion.3
  190.7 2.3 convolution_subtract_fusion.17
  193.0 11.7 %cholesky.504 = f32[128,128]{1,0:T(8,128)S(1)} custom-call(f32[128,128]{1,0:T(8,128)S(1)} %cholesky.596), custom_call_target="Cholesky" | custom-call | tf_op jit(solution)/shard_map/jit(cholesky)/cholesky | solution.py:45
  206.7 10.2 %custom-call.68 = f32[1,128,128]{1,2,0:T(8,128)S(1)} custom-call(f32[1,128,128]{2,1,0:T(8,128)S(1)} %get-tuple-element.53), custom_call_target="InvertDiagBlocksLowerTriangular" | custom-call | tf_op jit(solution)/shard_map/jit(cholesky)/cholesky | solution.py:45
  216.8 1.0 convolution_dynamic-update-slice_fusion.4
  217.9 2.3 convolution_subtract_fusion.18
  220.2 11.7 %cholesky.524 = f32[128,128]{1,0:T(8,128)S(1)} custom-call(f32[128,128]{1,0:T(8,128)S(1)} %cholesky.601), custom_call_target="Cholesky" | custom-call | tf_op jit(solution)/shard_map/jit(cholesky)/cholesky | solution.py:45
  233.8 9.8 %custom-call.69 = f32[1,128,128]{1,2,0:T(8,128)S(1)} custom-call(f32[1,128,128]{2,1,0:T(8,128)S(1)} %get-tuple-element.50), custom_call_target="InvertDiagBlocksLowerTriangular" | custom-call | tf_op jit(solution)/shard_map/jit(cholesky)/cholesky | solution.py:45
  243.6 0.9 convolution_dynamic-update-slice_fusion.5
  244.6 2.0 convolution_subtract_fusion.19
  246.6 11.9 %cholesky.544 = f32[128,128]{1,0:T(8,128)S(1)} custom-call(f32[128,128]{1,0:T(8,128)S(1)} %cholesky.606), custom_call_target="Cholesky" | custom-call | tf_op jit(solution)/shard_map/jit(cholesky)/cholesky | solution.py:45
  260.4 9.8 %custom-call.70 = f32[1,128,128]{1,2,0:T(8,128)S(1)} custom-call(f32[1,128,128]{2,1,0:T(8,128)S(1)} %get-tuple-element.47), custom_call_target="InvertDiagBlocksLowerTriangular" | custom-call | tf_op jit(solution)/shard_map/jit(cholesky)/cholesky | solution.py:45
  270.2 0.8 convolution_dynamic-update-slice_fusion.6
  271.0 1.8 convolution_subtract_fusion.20
  272.8 11.7 %cholesky.562 = f32[128,128]{1,0:T(8,128)S(1)} custom-call(f32[128,128]{1,0:T(8,128)S(1)} %convolution_subtract_fusion.20), custom_call_target="Cholesky" | custom-call | tf_op jit(solution)/shard_map/jit(cholesky)/cholesky | solution.py:45
  286.5 4.9 %select_select_fusion = f32[1024,1024]{1,0:T(8,128)} fusion(f32[1024,1024]{1,0:T(8,128)} %get-tuple-element.45, pred[]{:T(512)S(6)} %cholesky.576), kind=kLoop, calls=%fused_computation.3 | loop fusion | flops 4194304 | bytes 8388609 | tf_op jit(solution)/shard_map/triangular_solve | solution.py:11
  291.4 27.8 %while.1 = (s32[]{:T(128)}, f32[1024,1024]{1,0:T(8,128)}, s32[8,2]{0,1:T(2,128)S(1)}, f32[8,128,128]{2,1,0:T(8,128)}, s32[]{:T(128)}) while((s32[]{:T(128)}, f32[1024,1024]{1,0:T(8,128)}, s32[8,2]{0,1:T(2,128)S(1)}, f32[8,128,128]{2,1,0:T(8,128)}, s32[]{:T(128)}) %tuple.58), condition=%wide.while_cond, body=%wide.while_body.sunk | while | flops 2 | bytes 132205 | solution.py:11
  292.0 2.9 bitcast_dynamic-update-slice_fusion.2
  295.5 2.9 bitcast_dynamic-update-slice_fusion.2
  299.0 2.9 bitcast_dynamic-update-slice_fusion.2
  302.5 2.9 bitcast_dynamic-update-slice_fusion.2
  305.9 2.9 bitcast_dynamic-update-slice_fusion.2
  309.4 2.9 bitcast_dynamic-update-slice_fusion.2
  312.9 2.9 bitcast_dynamic-update-slice_fusion.2
  316.4 2.8 bitcast_dynamic-update-slice_fusion.2
  319.2 80.2 %custom-call.71 = f32[8,128,128]{1,2,0:T(8,128)} custom-call(f32[8,128,128]{2,1,0:T(8,128)} %get-tuple-element.12), custom_call_target="InvertDiagBlocksLowerTriangular" | custom-call | tf_op jit(solution)/shard_map/triangular_solve | solution.py:11
  399.4 1.3 constant_dynamic-update-slice_fusion.10
  400.8 1.6 convolution_subtract_fusion.10
  402.9 1.9 convolution_subtract_fusion.9
  405.2 1.5 convolution_subtract_fusion.14
  407.2 1.8 convolution_subtract_fusion.16
  409.5 2.3 convolution_subtract_fusion.8
  412.2 2.6 convolution_subtract_fusion.13
  415.2 3.3 convolution_subtract_fusion.7
  423.3 0.9 convolution_subtract_fusion.4
  424.8 1.1 convolution_subtract_fusion.11
  426.4 1.2 convolution_subtract_fusion.3
  428.2 1.4 fusion.107
  (97 shorter events, 25.8 us)
Async XLA Ops:
  0.0 3.5 copy-start
  81.3 1.9 copy-start.2
  286.5 114.3 %copy-start.3 = (f32[1024,512]{0,1:T(8,128)S(1)}, f32[1024,512]{0,1:T(8,128)}, u32[]{:S(2)}) copy-start(f32[1024,512]{0,1:T(8,128)} %get-tuple-element.23) | copy-start | bytes 6291460
  399.4 3.0 copy-start.4
  400.8 4.4 %copy-start.1 = (f32[1024,1024]{1,0:T(8,128)S(1)}, f32[1024,1024]{1,0:T(8,128)}, u32[]{:S(2)}) copy-start(f32[1024,1024]{1,0:T(8,128)} %get-tuple-element.130) | copy-start | bytes 12582916
where the time goes:
time: 434 us; the launch traced here: 430 us
  other arithmetic  266 us (61%)
  matrix products  58.7 us (14%)
  blocking collectives  57.7 us (13%)
  local copies, waits for them, and re-layouts  40.7 us (9%)
  between operations  6.96 us (2%)
    another operation x30, other arithmetic, local(): factor = jnp.linalg.cholesky(damped)  172 us
    another operation x3, other arithmetic, chol_solve(): lax.linalg.triangular_solve(factor, inner, left_side=True, lower=True, tr...  85.2 us
    all_gather x1, blocking collectives, local(): every_sk = lax.all_gather(local_sk, 'dp', axis=0, tiled=True)  30.5 us
    another operation x24, local copies, waits for them, and re-layouts  27.8 us
    psum x1, blocking collectives, local(): total_sq = lax.psum(jnp.sum(local_f32 * local_f32), 'dp')  23.4 us
    another operation x14, matrix products, local(): factor = jnp.linalg.cholesky(damped)  23.1 us
    another operation x15, matrix products, chol_solve(): inner = lax.linalg.triangular_solve(factor, rhs, left_side=True, lower=True)  19.4 us

commit v1 on v0

--- a/solution.py
+++ b/solution.py
@@ -1,9 +1,206 @@
 import jax
 import jax.numpy as jnp
 from jax import lax
+from jax.experimental import pallas as pl
+from jax.experimental.pallas import tpu as pltpu
 from jax.sharding import PartitionSpec as P
 
 E_DEV = 8
+LANES = 128
+NT = (((1,), (1,)), ((), ()))
+STEPS = ((4, 4), (3, 7), (1, 5), (2, 6))
+
+
+def chunks(size, parts):
+    per = -(-size // (parts * LANES)) * LANES
+    starts = range(0, size, per)
+    return [(s, min(per, size - s)) for s in starts]
+
+
+def project(acts, out_grads, in_t, out_t):
+    rin, rout = in_t.shape[0], out_t.shape[0]
+    tok = acts.shape[0]
+    a_cuts, g_cuts = chunks(acts.shape[1], 2), chunks(out_grads.shape[1], 4)
+
+    def kernel(a_hbm, g_hbm, i_hbm, o_hbm, out_ref, a_v, g_v, i_v, o_v, sems):
+        copies = []
+
+        def start(src, dst):
+            copy = pltpu.make_async_copy(src, dst, sems.at[len(copies)])
+            copy.start()
+            copies.append(copy)
+            return copy
+
+        i_copy = start(i_hbm, i_v)
+        a_copies = [start(a_hbm.at[:, pl.ds(s, n)], a_v.at[:, pl.ds(s, n)]) for s, n in a_cuts]
+        o_copy = start(o_hbm, o_v)
+        g_copies = [start(g_hbm.at[:, pl.ds(s, n)], g_v.at[:, pl.ds(s, n)]) for s, n in g_cuts]
+
+        def side(w_copy, w_v, x_copies, x_v, cuts):
+            w_copy.wait()
+            total = None
+            for copy, (s, n) in zip(x_copies, cuts):
+                copy.wait()
+                term = lax.dot_general(
+                    w_v[:, s : s + n], x_v[:, s : s + n], NT, preferred_element_type=jnp.float32
+                )
+                total = term if total is None else total + term
+            return total
+
+        out_ref[0:rin, :] = side(i_copy, i_v, a_copies, a_v, a_cuts)
+        out_ref[rin : rin + rout, :] = side(o_copy, o_v, g_copies, g_v, g_cuts)
+
+    hbm = pl.BlockSpec(memory_space=pl.ANY)
+    return pl.pallas_call(
+        kernel,
+        out_shape=jax.ShapeDtypeStruct((rin + rout, tok), jnp.float32),
+        in_specs=[hbm] * 4,
+        out_specs=pl.BlockSpec(memory_space=pltpu.VMEM),
+        scratch_shapes=[
+            pltpu.VMEM(acts.shape, acts.dtype),
+            pltpu.VMEM(out_grads.shape, out_grads.dtype),
+            pltpu.VMEM(in_t.shape, in_t.dtype),
+            pltpu.VMEM(out_t.shape, out_t.dtype),
+            pltpu.SemaphoreType.DMA((2 + len(a_cuts) + len(g_cuts),)),
+        ],
+        compiler_params=pltpu.CompilerParams(vmem_limit_bytes=16 * 2**20),
+        name="project",
+    )(acts, out_grads, in_t, out_t)
+
+
+def sketch(mine, other, ids, rin):
+    rout = mine.shape[0] - rin
+    tok = mine.shape[1]
+    groups = LANES // rin
+    o_per = rout // groups
+
+    def kernel(mine_ref, other_ref, ids_ref, out_ref):
+        both = (mine_ref[...] + other_ref[...]).astype(jnp.bfloat16)
+        left = both[0:rin]
+        right = both[rin : rin + rout].astype(jnp.float32)
+        member = lax.broadcasted_iota(jnp.int32, (E_DEV, tok), 0) == ids_ref[...]
+        member = jnp.where(member, 1.0, 0.0)
+        zero = jnp.zeros((rin, tok), jnp.bfloat16)
+        columns, rows = [], []
+        for g in range(groups):
+            masked = [member * right[g * o_per + o : g * o_per + o + 1] for o in range(o_per)]
+            columns.append(jnp.concatenate(masked, axis=0).astype(jnp.bfloat16))
+            rows.append(jnp.concatenate([left if h == g else zero for h in range(groups)], axis=1))
+        out_ref[...] = lax.dot_general(
+            jnp.concatenate(columns, axis=1),
+            jnp.concatenate(rows, axis=0),
+            NT,
+            preferred_element_type=jnp.float32,
+        ).astype(jnp.bfloat16)
+
+    return pl.pallas_call(
+        kernel,
+        out_shape=jax.ShapeDtypeStruct((o_per * E_DEV, LANES), jnp.bfloat16),
+        name="sketch",
+    )(mine, other, ids)
+
+
+def solve(blocks, owners, query_ids):
+    count = len(blocks)
+    size = count * E_DEV
+    k_size = blocks[0].shape[0] * LANES // E_DEV
+    queries = query_ids.shape[1]
+
+    def kernel(*refs):
+        block_refs, owner_ref, ids_ref, out_ref = refs[:count], refs[count], refs[count + 1], refs[count + 2]
+
+        def flat(ref):
+            block = ref[...].astype(jnp.float32)
+            cuts = [block[r : r + E_DEV] for r in range(0, block.shape[0], E_DEV)]
+            return jnp.concatenate(cuts, axis=1)
+
+        every = jnp.concatenate([flat(ref) for ref in block_refs], axis=0).astype(jnp.bfloat16)
+        twice = jnp.concatenate([every, every], axis=0)
+        gram = lax.dot_general(every, twice, NT, preferred_element_type=jnp.float32)
+        row = lax.broadcasted_iota(jnp.int32, (size, 2 * size), 0)
+        lane = lax.broadcasted_iota(jnp.int32, (size, 2 * size), 1)
+        diagonal = row == lane
+        damping = 0.1 * jnp.sum(jnp.where(diagonal, gram, 0.0)) / k_size
+        right_eye = jnp.where(row + size == lane, 1.0, 0.0)
+        system = jnp.where(lane < size, gram + jnp.where(diagonal, damping, 0.0), right_eye)
+        table = [system[r : r + E_DEV] for r in range(0, size, E_DEV)]
+        shape = table[0].shape
+        sub = lax.broadcasted_iota(jnp.int32, shape, 0)
+
+        def down(value, i):
+            return jnp.broadcast_to(value[i : i + 1], shape)
+
+        for k in range(count):
+            wide = [[jnp.broadcast_to(t[:, c : c + 1], shape) for c in range(k * E_DEV, (k + 1) * E_DEV)] for t in table]
+            pivot, cols = table[k], wide[k]
+            for i in range(E_DEV):
+                scale = 1.0 / down(cols[i], i)
+                here = sub == i
+                factor = cols[i]
+
+                def clear(value):
+                    line = down(value, i) * scale
+                    return jnp.where(here, line, value - factor * line)
+
+                pivot = clear(pivot)
+                cols = [clear(c) if j > i else c for j, c in enumerate(cols)]
+            table[k] = pivot
+            lines = [down(pivot, j) for j in range(E_DEV)]
+            for r in range(count):
+                if r != k:
+                    drop = wide[r][0] * lines[0]
+                    for j in range(1, E_DEV):
+                        drop = drop + wide[r][j] * lines[j]
+                    table[r] = table[r] - drop
+        eye = jnp.where(sub + size == lane[0:E_DEV], 1.0, 0.0)
+        result = jnp.where(lane[0:E_DEV] >= size, eye - damping * table[0], 0.0)
+
+        spot = lax.broadcasted_iota(jnp.int32, (2 * size, queries), 0)
+        place = (spot - size) // E_DEV
+        example = jnp.full_like(spot, -1)
+        for b in range(count):
+            example = jnp.where(place == b, owner_ref[b] * E_DEV, example)
+        example = example + spot % E_DEV
+        chosen = jnp.where((spot >= size) & (example == ids_ref[...]), 1.0, 0.0).astype(jnp.bfloat16)
+        high = result.astype(jnp.bfloat16)
+        rest = result - high.astype(jnp.float32)
+        mid = rest.astype(jnp.bfloat16)
+        low = (rest - mid.astype(jnp.float32)).astype(jnp.bfloat16)
+        picks = [jnp.dot(part, chosen, preferred_element_type=jnp.float32) for part in (high, mid, low)]
+        out_ref[...] = picks[0] + (picks[1] + picks[2])
+
+    vmem = pl.BlockSpec(memory_space=pltpu.VMEM)
+    return pl.pallas_call(
+        kernel,
+        out_shape=jax.ShapeDtypeStruct((E_DEV, queries), jnp.float32),
+        in_specs=[vmem] * count + [pl.BlockSpec(memory_space=pltpu.SMEM), vmem],
+        out_specs=vmem,
+        name="solve",
+    )(*blocks, owners, query_ids)
+
+
+def fetch(value, pair, count):
+    moves = [(2 * i + c, 2 * (i ^ pair[c]) + c) for i in range(count) for c in range(2)]
+    return lax.ppermute(value, ("dp", "mp"), moves)
+
+
+def swap(value):
+    return lax.ppermute(value, "mp", [(0, 1), (1, 0)])
+
+
+def local_small(acts, out_grads, in_proj, out_proj, example_ids, query_ids):
+    count = lax.axis_size("dp")
+    mine = project(acts, out_grads, in_proj.T, out_proj.T)
+    own = sketch(mine, swap(mine), example_ids, in_proj.shape[1])
+    near = [fetch(own, pair, count) for pair in STEPS]
+    far = [swap(block) for block in near[1:]]
+    core = lax.axis_index("mp")
+    steps = jnp.array(
+        [[0] + [p[c] for p in STEPS] + [p[1 - c] for p in STEPS[1:]] for c in range(2)], jnp.int32
+    )
+    owners = steps[core] ^ lax.axis_index("dp")
+    picked = solve([own] + near + far, owners, query_ids.reshape(1, -1))
+    return picked.T
 
 
 def chol_solve(factor, rhs):
@@ -11,7 +208,7 @@
     return lax.linalg.triangular_solve(factor, inner, left_side=True, lower=True, transpose_a=True)
 
 
-def local(acts, out_grads, in_proj, out_proj, example_ids, query_ids):
+def local_large(acts, out_grads, in_proj, out_proj, example_ids, query_ids):
     part_in = jnp.dot(acts, in_proj, preferred_element_type=jnp.float32)
     part_out = jnp.dot(out_grads, out_proj, preferred_element_type=jnp.float32)
     full_in, full_out = lax.psum((part_in, part_out), "mp")
@@ -20,18 +217,17 @@
     tok_count = left.shape[0]
     rin_size = left.shape[1]
     rout_size = right.shape[1]
-    ex_count = E_DEV
     k_size = rin_size * rout_size
     ids = example_ids[0]
-    onehot = (ids[:, None] == jnp.arange(ex_count, dtype=jnp.int32)[None, :]).astype(jnp.bfloat16)
-    wide = (onehot[:, :, None] * left[:, None, :]).reshape(tok_count, ex_count * rin_size)
+    onehot = (ids[:, None] == jnp.arange(E_DEV, dtype=jnp.int32)[None, :]).astype(jnp.bfloat16)
+    wide = (onehot[:, :, None] * left[:, None, :]).reshape(tok_count, E_DEV * rin_size)
     summed = lax.dot_general(
         right, wide, (((0,), (0,)), ((), ())), preferred_element_type=jnp.float32
     )
     local_sk = (
-        summed.reshape(rout_size, ex_count, rin_size)
+        summed.reshape(rout_size, E_DEV, rin_size)
         .transpose(1, 0, 2)
-        .reshape(ex_count, k_size)
+        .reshape(E_DEV, k_size)
         .astype(jnp.bfloat16)
     )
     every_sk = lax.all_gather(local_sk, "dp", axis=0, tiled=True)
@@ -60,4 +256,6 @@
         P(("groups", "mp")),
     )
     out_specs = P(("groups", "mp"), "dp")
+    small = mesh.shape["dp"] == 8 and mesh.shape["mp"] == 2
+    local = local_small if small else local_large
     return jax.shard_map(local, mesh=mesh, in_specs=in_specs, out_specs=out_specs, check_vma=False)

time: 434 us -> 26.2 us (0.06)
  other arithmetic: 266 us -> 0.54 us
  matrix products: 58.7 us -> 0 us
  blocking collectives: 57.7 us -> 0 us
  local copies, waits for them, and re-layouts: 40.7 us -> 5.5 us
  starting transfers between devices: 0 us -> 10.9 us
  Pallas kernels: 0 us -> 7.66 us
  between operations: 6.96 us -> 0.07 us
    another operation x33 -> x0, other arithmetic: 257 us -> none  [the longest x30 172 us: local(): factor = jnp.linalg.cholesky(damped)]
    another operation x44 -> x0, matrix products: 51 us -> none  [the longest x14 23.1 us: local(): factor = jnp.linalg.cholesky(damped)]
    all_gather x1 -> x0, blocking collectives: 30.5 us -> none  [local(): every_sk = lax.all_gather(local_sk, 'dp', axis=0, tiled=True)]
    another operation x37 -> x0, local copies, waits for them, and re-layouts: 30.4 us -> none
    psum x2 -> x0, blocking collectives: 27.1 us -> none  [the longest x1 23.4 us: local(): total_sq = lax.psum(jnp.sum(local_f32 * local_f32), 'dp')]
    ppermute x0 -> x8, starting transfers between devices: none -> 10.9 us  [the longest x4 7.42 us: fetch(): return lax.ppermute(value, ('dp', 'mp'), moves)]
    dot_general x5 -> x0, matrix products: 7.73 us -> none  [the longest x1 2.66 us: local(): lax.dot_general(every_sk, every_sk, (((0,), (0,)), ((), ())), preferred_e...]
    pallas_call x0 -> x3, Pallas kernels: none -> 7.66 us  [the longest x1 4.12 us: solve(): pl.pallas_call(kernel, out_shape=jax.ShapeDtypeStruct((E_DEV, queries), j...]
  transfers between devices with their start and end apart: 0 -> 8, of which waited for: 0 -> 2; matrix products, arithmetic and copies ran while one was open for 0% -> 2% of each run, Pallas kernels for 0% -> 0%
where the time goes in v1:
time: 26.2 us; the launch traced here: 25.8 us
  starting transfers between devices  10.9 us (42%)
  Pallas kernels  7.66 us (29%)
  local copies, waits for them, and re-layouts  5.5 us (21%)
  waiting for transfers between devices  1.13 us (4%)
  other arithmetic  0.54 us (2%)
    ppermute x4, starting transfers between devices, fetch(): return lax.ppermute(value, ('dp', 'mp'), moves)  7.42 us
    unnamed x28, local copies, waits for them, and re-layouts  5.5 us
    pallas_call x1, Pallas kernels, solve(): pl.pallas_call(kernel, out_shape=jax.ShapeDtypeStruct((E_DEV, queries), j...  4.12 us
    ppermute x4, starting transfers between devices, swap(): return lax.ppermute(value, 'mp', [(0, 1), (1, 0)])  3.5 us
    pallas_call x1, Pallas kernels, project(): pl.pallas_call(kernel, out_shape=jax.ShapeDtypeStruct((rin + rout, tok),...  2 us
    pallas_call x1, Pallas kernels, sketch(): pl.pallas_call(kernel, out_shape=jax.ShapeDtypeStruct((o_per * E_DEV, LAN...  1.54 us
    ppermute x4, waiting for transfers between devices, swap(): return lax.ppermute(value, 'mp', [(0, 1), (1, 0)])  1.12 us
    xor x1, other arithmetic, local_small(): owners = steps[core] ^ lax.axis_index('dp')  0.54 us
  transfers between devices with their start and end apart: 8, of which 2 were waited for; matrix products, arithmetic and copies ran while one was open for 2% of the time, Pallas kernels for 0%

profile of v1, /device:TPU:0, one launch (start us, length us, event | category | flops | bytes accessed | tf_op | source)
XLA Modules:
  0.0 25.8 jit_solution(1328676389004027364)
XLA Ops:
  0.0 0.0 copy-start.13
  0.0 0.0 copy-start
  0.0 1.4 %copy-done = bf16[128,5504]{1,0:T(8,128)(2,1)S(1)} copy-done((bf16[128,5504]{1,0:T(8,128)(2,1)S(1)}, bf16[128,5504]{1,0:T(8,128)(2,1)}, u32[]{:S(2)}) %copy-start) | copy-done | bytes 1409048
  1.4 0.0 copy-start.1
  1.4 1.0 %copy-done.1 = bf16[128,2048]{1,0:T(8,128)(2,1)S(1)} copy-done((bf16[128,2048]{1,0:T(8,128)(2,1)S(1)}, bf16[128,2048]{1,0:T(8,128)(2,1)}, u32[]{:S(2)}) %copy-start.1) | copy-done | bytes 524312
  2.4 0.0 copy-start.2
  2.4 1.0 %copy-done.2 = bf16[5504,32]{0,1:T(8,128)(2,1)S(1)} copy-done((bf16[5504,32]{0,1:T(8,128)(2,1)S(1)}, bf16[5504,32]{0,1:T(8,128)(2,1)}, u32[]{:S(2)}) %copy-start.2) | copy-done | bytes 352280
  3.4 0.0 copy-start.4
  3.4 0.9 %copy-done.4 = bf16[2048,32]{0,1:T(8,128)(2,1)S(1)} copy-done((bf16[2048,32]{0,1:T(8,128)(2,1)S(1)}, bf16[2048,32]{0,1:T(8,128)(2,1)}, u32[]{:S(2)}) %copy-start.4) | copy-done | bytes 131096
  4.3 2.0 %project.1.mine_ref = f32[64,128]{1,0:T(8,128)S(1)} custom-call(bf16[128,2048]{1,0:T(8,128)(2,1)S(1)} %copy-done.1, bf16[128,5504]{1,0:T(8,128)(2,1)S(1)} %copy-done, bf16[32,2048]{1,0:T(8,128)(2,1)S(1)} %bitcast.7, bf16[32,5504]{1,0:T(8,128)(2,1)S(1)} %bitcast.6), custom_call_target="tpu_custom_call" | custom-call | tf_op jit(solution)/shard_map/project/pallas_call | solution.py:54
  6.3 0.0 copy-start.3
  6.3 0.5 %collective-permute-start = (f32[64,128]{1,0:T(8,128)S(1)}, f32[64,128]{1,0:T(8,128)S(1)}, u32[]{:S(2)}, u32[]{:S(2)}) collective-permute-start(f32[64,128]{1,0:T(8,128)S(1)} %project.1.mine_ref), channel_id=1, source_target_pairs={{0,1},{1,0},{2,3},{3,2},{4,5},{5,4},{6,7},{7,6},{8,9},{9,8},{10,11... | collective-permute-start | bytes 98312 | tf_op jit(solution)/shard_map/ppermute | solution.py:188
  6.8 0.9 %collective-permute-done.other_ref = f32[64,128]{1,0:T(8,128)S(1)} collective-permute-done((f32[64,128]{1,0:T(8,128)S(1)}, f32[64,128]{1,0:T(8,128)S(1)}, u32[]{:S(2)}, u32[]{:S(2)}) %collective-permute-start) | collective-permute-done | bytes 32800 | tf_op jit(solution)/shard_map/ppermute | solution.py:188
  7.7 0.0 copy-done.3
  7.7 0.0 copy-start.5
  7.7 0.6 %copy-done.5 = f32[64,128]{1,0:T(8,128)} copy-done((f32[64,128]{1,0:T(8,128)}, f32[64,128]{1,0:T(8,128)S(1)}, u32[]{:S(2)}) %copy-start.5) | copy-done | bytes 32792
  8.3 1.5 %sketch.1.refs_0_ = bf16[64,128]{1,0:T(8,128)(2,1)} custom-call(f32[64,128]{1,0:T(8,128)} %copy-done.3, f32[64,128]{1,0:T(8,128)} %copy-done.5, s32[1,128]{1,0:T(1,128)} %ids_ref.1), custom_call_target="tpu_custom_call" | custom-call | tf_op jit(solution)/shard_map/sketch/pallas_call | solution.py:96
  9.8 2.9 %collective-permute-start.4 = (bf16[64,128]{1,0:T(8,128)(2,1)}, bf16[64,128]{1,0:T(8,128)(2,1)S(1)}, u32[]{:S(2)}, u32[]{:S(2)}) collective-permute-start(bf16[64,128]{1,0:T(8,128)(2,1)} %sketch.1.refs_0_), channel_id=1, source_target_pairs={{0,4},{1,13},{2,6},{3,15},{4,0},{5,9},{6,2},{7,11},{8,12},{9,5},{1... | collective-permute-start | bytes 49160 | tf_op jit(solution)/shard_map/ppermute | solution.py:184
  12.8 1.5 %collective-permute-start.3 = (bf16[64,128]{1,0:T(8,128)(2,1)}, bf16[64,128]{1,0:T(8,128)(2,1)S(1)}, u32[]{:S(2)}, u32[]{:S(2)}) collective-permute-start(bf16[64,128]{1,0:T(8,128)(2,1)} %sketch.1.refs_0_), channel_id=1, source_target_pairs={{0,2},{1,11},{2,0},{3,9},{4,6},{5,15},{6,4},{7,13},{8,10},{9,3},{1... | collective-permute-start | bytes 49160 | tf_op jit(solution)/shard_map/ppermute | solution.py:184
  14.2 0.0 collective-permute-start.2
  14.3 3.0 %collective-permute-start.1 = (bf16[64,128]{1,0:T(8,128)(2,1)}, bf16[64,128]{1,0:T(8,128)(2,1)S(1)}, u32[]{:S(2)}, u32[]{:S(2)}) collective-permute-start(bf16[64,128]{1,0:T(8,128)(2,1)} %sketch.1.refs_0_), channel_id=1, source_target_pairs={{0,8},{1,9},{2,10},{3,11},{4,12},{5,13},{6,14},{7,15},{8,0},{9,1},... | collective-permute-start | bytes 49160 | tf_op jit(solution)/shard_map/ppermute | solution.py:184
  17.3 0.0 collective-permute-done.4.refs_4_
  17.3 0.0 copy-start.6
  17.3 0.7 %collective-permute-start.7 = (bf16[64,128]{1,0:T(8,128)(2,1)S(1)}, bf16[64,128]{1,0:T(8,128)(2,1)S(1)}, u32[]{:S(2)}, u32[]{:S(2)}) collective-permute-start(bf16[64,128]{1,0:T(8,128)(2,1)S(1)} %collective-permute-done.4.refs_4_), channel_id=1, source_target_pairs={{0,1},{1,0},{2,3},{3,2},{4,5},{5,4},{6,7},{7,6},{8,9},{9,8},{10,11... | collective-permute-start | bytes 49160 | tf_op jit(solution)/shard_map/ppermute | solution.py:188
  18.0 0.0 collective-permute-done.3.refs_3_
  18.0 0.0 copy-start.7
  18.0 1.3 %collective-permute-start.6 = (bf16[64,128]{1,0:T(8,128)(2,1)S(1)}, bf16[64,128]{1,0:T(8,128)(2,1)S(1)}, u32[]{:S(2)}, u32[]{:S(2)}) collective-permute-start(bf16[64,128]{1,0:T(8,128)(2,1)S(1)} %collective-permute-done.3.refs_3_), channel_id=1, source_target_pairs={{0,1},{1,0},{2,3},{3,2},{4,5},{5,4},{6,7},{7,6},{8,9},{9,8},{10,11... | collective-permute-start | bytes 49160 | tf_op jit(solution)/shard_map/ppermute | solution.py:188
  19.3 0.0 collective-permute-done.2.refs_2_
  19.3 0.0 copy-start.8
  19.3 1.0 %collective-permute-start.5 = (bf16[64,128]{1,0:T(8,128)(2,1)S(1)}, bf16[64,128]{1,0:T(8,128)(2,1)S(1)}, u32[]{:S(2)}, u32[]{:S(2)}) collective-permute-start(bf16[64,128]{1,0:T(8,128)(2,1)S(1)} %collective-permute-done.2.refs_2_), channel_id=1, source_target_pairs={{0,1},{1,0},{2,3},{3,2},{4,5},{5,4},{6,7},{7,6},{8,9},{9,8},{10,11... | collective-permute-start | bytes 49160 | tf_op jit(solution)/shard_map/ppermute | solution.py:188
  20.3 0.0 copy-done.13
  20.3 0.5 %xor_bitcast_fusion.refs_8_ = s32[8]{0:T(128)} fusion(s32[2,8]{1,0:T(2,128)S(1)} %copy-done.13, s32[]{:T(128)S(6)} %select_n.3, s32[]{:T(128)S(6)} %axis_index.25), kind=kLoop, calls=%fused_computation | loop fusion | flops 8 | bytes 72 | tf_op jit(solution)/shard_map/xor | solution.py:201
  20.8 0.0 collective-permute-done.1.refs_1_
  20.8 0.0 copy-start.9
  20.8 0.0 collective-permute-done.7.refs_7_
  20.8 0.0 copy-start.10
  20.8 0.0 collective-permute-done.6.refs_6_
  20.8 0.0 copy-start.11
  20.8 0.3 collective-permute-done.5.refs_5_
  21.1 0.0 copy-start.12
  21.1 0.0 copy-done.6
  21.1 0.0 copy-done.7
  21.1 0.0 copy-done.8
  21.1 0.3 %copy-done.9 = bf16[64,128]{1,0:T(8,128)(2,1)} copy-done((bf16[64,128]{1,0:T(8,128)(2,1)}, bf16[64,128]{1,0:T(8,128)(2,1)S(1)}, u32[]{:S(2)}) %copy-start.9) | copy-done | bytes 16408
  21.4 0.0 copy-done.10
  21.4 0.0 copy-done.11
  21.4 0.3 %copy-done.12 = bf16[64,128]{1,0:T(8,128)(2,1)} copy-done((bf16[64,128]{1,0:T(8,128)(2,1)}, bf16[64,128]{1,0:T(8,128)(2,1)S(1)}, u32[]{:S(2)}) %copy-start.12) | copy-done | bytes 16408
  21.7 4.1 %solve.1 = f32[8,512]{1,0:T(8,128)} custom-call(bf16[64,128]{1,0:T(8,128)(2,1)} %sketch.1.refs_0_, bf16[64,128]{1,0:T(8,128)(2,1)} %copy-done.9, bf16[64,128]{1,0:T(8,128)(2,1)} %copy-done.8, bf16[64,128]{1,0:T(8,128)(2,1)} %copy-done.7, bf16[64,128]{1,0:T(8,128)(2,1)} %copy-done.6, bf16[64,128]{1,0:T(8,128)(2,1)} %copy-done.12, bf16[64,128]{1,0:T(8,128)(2,1)} %copy-done.11, ...), custom_call_target="tpu_custom_call" | custom-call | tf_op jit(solution)/shard_map/solve/pallas_call | solution.py:173
Async XLA Ops:
  0.0 20.3 %copy-start.13 = (s32[2,8]{1,0:T(2,128)S(1)}, s32[2,8]{1,0:T(2,128)}, u32[]{:S(2)}) copy-start(s32[2,8]{1,0:T(2,128)} %constant.14.clone) | copy-start | bytes 196
  0.0 1.4 %copy-start = (bf16[128,5504]{1,0:T(8,128)(2,1)S(1)}, bf16[128,5504]{1,0:T(8,128)(2,1)}, u32[]{:S(2)}) copy-start(bf16[128,5504]{1,0:T(8,128)(2,1)} %g_hbm.1) | copy-start | bytes 4227076
  1.4 1.0 %copy-start.1 = (bf16[128,2048]{1,0:T(8,128)(2,1)S(1)}, bf16[128,2048]{1,0:T(8,128)(2,1)}, u32[]{:S(2)}) copy-start(bf16[128,2048]{1,0:T(8,128)(2,1)} %a_hbm.1) | copy-start | bytes 1572868
  2.4 1.0 %copy-start.2 = (bf16[5504,32]{0,1:T(8,128)(2,1)S(1)}, bf16[5504,32]{0,1:T(8,128)(2,1)}, u32[]{:S(2)}) copy-start(bf16[5504,32]{0,1:T(8,128)(2,1)} %param.10) | copy-start | bytes 1056772
  3.4 0.9 %copy-start.4 = (bf16[2048,32]{0,1:T(8,128)(2,1)S(1)}, bf16[2048,32]{0,1:T(8,128)(2,1)}, u32[]{:S(2)}) copy-start(bf16[2048,32]{0,1:T(8,128)(2,1)} %param.9) | copy-start | bytes 393220
  6.3 1.4 %copy-start.3 = (f32[64,128]{1,0:T(8,128)}, f32[64,128]{1,0:T(8,128)S(1)}, u32[]{:S(2)}) copy-start(f32[64,128]{1,0:T(8,128)S(1)} %project.1.mine_ref) | copy-start | bytes 98308
  6.3 1.4 %collective-permute-start = (f32[64,128]{1,0:T(8,128)S(1)}, f32[64,128]{1,0:T(8,128)S(1)}, u32[]{:S(2)}, u32[]{:S(2)}) collective-permute-start(f32[64,128]{1,0:T(8,128)S(1)} %project.1.mine_ref), channel_id=1, source_target_pairs={{0,1},{1,0},{2,3},{3,2},{4,5},{5,4},{6,7},{7,6},{8,9},{9,8},{10,11... | collective-permute-start | bytes 98312 | tf_op jit(solution)/shard_map/ppermute | solution.py:188
  7.7 0.6 %copy-start.5 = (f32[64,128]{1,0:T(8,128)}, f32[64,128]{1,0:T(8,128)S(1)}, u32[]{:S(2)}) copy-start(f32[64,128]{1,0:T(8,128)S(1)} %collective-permute-done.other_ref) | copy-start | bytes 98308
  9.8 7.4 %collective-permute-start.4 = (bf16[64,128]{1,0:T(8,128)(2,1)}, bf16[64,128]{1,0:T(8,128)(2,1)S(1)}, u32[]{:S(2)}, u32[]{:S(2)}) collective-permute-start(bf16[64,128]{1,0:T(8,128)(2,1)} %sketch.1.refs_0_), channel_id=1, source_target_pairs={{0,4},{1,13},{2,6},{3,15},{4,0},{5,9},{6,2},{7,11},{8,12},{9,5},{1... | collective-permute-start | bytes 49160 | tf_op jit(solution)/shard_map/ppermute | solution.py:184
  12.8 5.2 %collective-permute-start.3 = (bf16[64,128]{1,0:T(8,128)(2,1)}, bf16[64,128]{1,0:T(8,128)(2,1)S(1)}, u32[]{:S(2)}, u32[]{:S(2)}) collective-permute-start(bf16[64,128]{1,0:T(8,128)(2,1)} %sketch.1.refs_0_), channel_id=1, source_target_pairs={{0,2},{1,11},{2,0},{3,9},{4,6},{5,15},{6,4},{7,13},{8,10},{9,3},{1... | collective-permute-start | bytes 49160 | tf_op jit(solution)/shard_map/ppermute | solution.py:184
  14.2 5.0 %collective-permute-start.2 = (bf16[64,128]{1,0:T(8,128)(2,1)}, bf16[64,128]{1,0:T(8,128)(2,1)S(1)}, u32[]{:S(2)}, u32[]{:S(2)}) collective-permute-start(bf16[64,128]{1,0:T(8,128)(2,1)} %sketch.1.refs_0_), channel_id=1, source_target_pairs={{0,6},{1,15},{2,4},{3,13},{4,2},{5,11},{6,0},{7,9},{8,14},{9,7},{1... | collective-permute-start | bytes 49160 | tf_op jit(solution)/shard_map/ppermute | solution.py:184
  14.3 6.6 %collective-permute-start.1 = (bf16[64,128]{1,0:T(8,128)(2,1)}, bf16[64,128]{1,0:T(8,128)(2,1)S(1)}, u32[]{:S(2)}, u32[]{:S(2)}) collective-permute-start(bf16[64,128]{1,0:T(8,128)(2,1)} %sketch.1.refs_0_), channel_id=1, source_target_pairs={{0,8},{1,9},{2,10},{3,11},{4,12},{5,13},{6,14},{7,15},{8,0},{9,1},... | collective-permute-start | bytes 49160 | tf_op jit(solution)/shard_map/ppermute | solution.py:184
  17.3 3.8 %copy-start.6 = (bf16[64,128]{1,0:T(8,128)(2,1)}, bf16[64,128]{1,0:T(8,128)(2,1)S(1)}, u32[]{:S(2)}) copy-start(bf16[64,128]{1,0:T(8,128)(2,1)S(1)} %collective-permute-done.4.refs_4_) | copy-start | bytes 49156
  17.3 3.5 %collective-permute-start.7 = (bf16[64,128]{1,0:T(8,128)(2,1)S(1)}, bf16[64,128]{1,0:T(8,128)(2,1)S(1)}, u32[]{:S(2)}, u32[]{:S(2)}) collective-permute-start(bf16[64,128]{1,0:T(8,128)(2,1)S(1)} %collective-permute-done.4.refs_4_), channel_id=1, source_target_pairs={{0,1},{1,0},{2,3},{3,2},{4,5},{5,4},{6,7},{7,6},{8,9},{9,8},{10,11... | collective-permute-start | bytes 49160 | tf_op jit(solution)/shard_map/ppermute | solution.py:188
  18.0 3.1 %copy-start.7 = (bf16[64,128]{1,0:T(8,128)(2,1)}, bf16[64,128]{1,0:T(8,128)(2,1)S(1)}, u32[]{:S(2)}) copy-start(bf16[64,128]{1,0:T(8,128)(2,1)S(1)} %collective-permute-done.3.refs_3_) | copy-start | bytes 49156
  18.0 2.9 %collective-permute-start.6 = (bf16[64,128]{1,0:T(8,128)(2,1)S(1)}, bf16[64,128]{1,0:T(8,128)(2,1)S(1)}, u32[]{:S(2)}, u32[]{:S(2)}) collective-permute-start(bf16[64,128]{1,0:T(8,128)(2,1)S(1)} %collective-permute-done.3.refs_3_), channel_id=1, source_target_pairs={{0,1},{1,0},{2,3},{3,2},{4,5},{5,4},{6,7},{7,6},{8,9},{9,8},{10,11... | collective-permute-start | bytes 49160 | tf_op jit(solution)/shard_map/ppermute | solution.py:188
  19.3 1.8 %copy-start.8 = (bf16[64,128]{1,0:T(8,128)(2,1)}, bf16[64,128]{1,0:T(8,128)(2,1)S(1)}, u32[]{:S(2)}) copy-start(bf16[64,128]{1,0:T(8,128)(2,1)S(1)} %collective-permute-done.2.refs_2_) | copy-start | bytes 49156
  19.3 1.8 %collective-permute-start.5 = (bf16[64,128]{1,0:T(8,128)(2,1)S(1)}, bf16[64,128]{1,0:T(8,128)(2,1)S(1)}, u32[]{:S(2)}, u32[]{:S(2)}) collective-permute-start(bf16[64,128]{1,0:T(8,128)(2,1)S(1)} %collective-permute-done.2.refs_2_), channel_id=1, source_target_pairs={{0,1},{1,0},{2,3},{3,2},{4,5},{5,4},{6,7},{7,6},{8,9},{9,8},{10,11... | collective-permute-start | bytes 49160 | tf_op jit(solution)/shard_map/ppermute | solution.py:188
  20.8 0.6 %copy-start.9 = (bf16[64,128]{1,0:T(8,128)(2,1)}, bf16[64,128]{1,0:T(8,128)(2,1)S(1)}, u32[]{:S(2)}) copy-start(bf16[64,128]{1,0:T(8,128)(2,1)S(1)} %collective-permute-done.1.refs_1_) | copy-start | bytes 49156
  20.8 0.6 %copy-start.10 = (bf16[64,128]{1,0:T(8,128)(2,1)}, bf16[64,128]{1,0:T(8,128)(2,1)S(1)}, u32[]{:S(2)}) copy-start(bf16[64,128]{1,0:T(8,128)(2,1)S(1)} %collective-permute-done.7.refs_7_) | copy-start | bytes 49156
  20.8 0.6 %copy-start.11 = (bf16[64,128]{1,0:T(8,128)(2,1)}, bf16[64,128]{1,0:T(8,128)(2,1)S(1)}, u32[]{:S(2)}) copy-start(bf16[64,128]{1,0:T(8,128)(2,1)S(1)} %collective-permute-done.6.refs_6_) | copy-start | bytes 49156
  21.1 0.6 %copy-start.12 = (bf16[64,128]{1,0:T(8,128)(2,1)}, bf16[64,128]{1,0:T(8,128)(2,1)S(1)}, u32[]{:S(2)}) copy-start(bf16[64,128]{1,0:T(8,128)(2,1)S(1)} %collective-permute-done.5.refs_5_) | copy-start | bytes 49156

commit v2 on v1

--- a/solution.py
+++ b/solution.py
@@ -9,6 +9,7 @@
 LANES = 128
 NT = (((1,), (1,)), ((), ()))
 STEPS = ((4, 4), (3, 7), (1, 5), (2, 6))
+ORDER = ((0, 0),) + STEPS + tuple((b, a) for a, b in STEPS[1:])
 
 
 def chunks(size, parts):
@@ -17,12 +18,12 @@
     return [(s, min(per, size - s)) for s in starts]
 
 
-def project(acts, out_grads, in_t, out_t):
+def project(acts, out_grads, in_t, out_t, example_ids, query_ids):
     rin, rout = in_t.shape[0], out_t.shape[0]
     tok = acts.shape[0]
-    a_cuts, g_cuts = chunks(acts.shape[1], 2), chunks(out_grads.shape[1], 4)
-
-    def kernel(a_hbm, g_hbm, i_hbm, o_hbm, out_ref, a_v, g_v, i_v, o_v, sems):
+    g_cuts = chunks(out_grads.shape[1], 2)
+
+    def kernel(a_hbm, g_hbm, i_hbm, o_hbm, e_hbm, q_hbm, out_ref, e_ref, q_ref, a_v, g_v, i_v, o_v, sems):
         copies = []
 
         def start(src, dst):
@@ -32,40 +33,46 @@
             return copy
 
         i_copy = start(i_hbm, i_v)
-        a_copies = [start(a_hbm.at[:, pl.ds(s, n)], a_v.at[:, pl.ds(s, n)]) for s, n in a_cuts]
+        a_copy = start(a_hbm, a_v)
         o_copy = start(o_hbm, o_v)
         g_copies = [start(g_hbm.at[:, pl.ds(s, n)], g_v.at[:, pl.ds(s, n)]) for s, n in g_cuts]
-
-        def side(w_copy, w_v, x_copies, x_v, cuts):
-            w_copy.wait()
-            total = None
-            for copy, (s, n) in zip(x_copies, cuts):
-                copy.wait()
-                term = lax.dot_general(
-                    w_v[:, s : s + n], x_v[:, s : s + n], NT, preferred_element_type=jnp.float32
-                )
-                total = term if total is None else total + term
-            return total
-
-        out_ref[0:rin, :] = side(i_copy, i_v, a_copies, a_v, a_cuts)
-        out_ref[rin : rin + rout, :] = side(o_copy, o_v, g_copies, g_v, g_cuts)
-
-    hbm = pl.BlockSpec(memory_space=pl.ANY)
+        e_copy = start(e_hbm, e_ref)
+        q_copy = start(q_hbm, q_ref)
+        i_copy.wait()
+        a_copy.wait()
+        out_ref[0:rin, :] = lax.dot_general(i_v[...], a_v[...], NT, preferred_element_type=jnp.float32)
+        o_copy.wait()
+        total = None
+        for copy, (s, n) in zip(g_copies, g_cuts):
+            copy.wait()
+            term = lax.dot_general(o_v[:, s : s + n], g_v[:, s : s + n], NT, preferred_element_type=jnp.float32)
+            total = term if total is None else total + term
+        out_ref[rin : rin + rout, :] = total
+        e_copy.wait()
+        q_copy.wait()
+
+    hbm = pl.BlockSpec(memory_space=pltpu.HBM)
+    vmem = pl.BlockSpec(memory_space=pltpu.VMEM)
+    operands = (acts, out_grads, in_t, out_t, example_ids, query_ids)
     return pl.pallas_call(
         kernel,
-        out_shape=jax.ShapeDtypeStruct((rin + rout, tok), jnp.float32),
-        in_specs=[hbm] * 4,
-        out_specs=pl.BlockSpec(memory_space=pltpu.VMEM),
+        out_shape=[
+            jax.ShapeDtypeStruct((rin + rout, tok), jnp.float32),
+            jax.ShapeDtypeStruct(example_ids.shape, example_ids.dtype),
+            jax.ShapeDtypeStruct(query_ids.shape, query_ids.dtype),
+        ],
+        in_specs=[hbm] * 6,
+        out_specs=[vmem] * 3,
         scratch_shapes=[
             pltpu.VMEM(acts.shape, acts.dtype),
             pltpu.VMEM(out_grads.shape, out_grads.dtype),
             pltpu.VMEM(in_t.shape, in_t.dtype),
             pltpu.VMEM(out_t.shape, out_t.dtype),
-            pltpu.SemaphoreType.DMA((2 + len(a_cuts) + len(g_cuts),)),
+            pltpu.SemaphoreType.DMA((5 + len(g_cuts),)),
         ],
         compiler_params=pltpu.CompilerParams(vmem_limit_bytes=16 * 2**20),
         name="project",
-    )(acts, out_grads, in_t, out_t)
+    )(*[pltpu.with_memory_space_constraint(x, pltpu.HBM) for x in operands])
 
 
 def sketch(mine, other, ids, rin):
@@ -96,18 +103,19 @@
     return pl.pallas_call(
         kernel,
         out_shape=jax.ShapeDtypeStruct((o_per * E_DEV, LANES), jnp.bfloat16),
+        compiler_params=pltpu.CompilerParams(vmem_limit_bytes=4 * 2**20),
         name="sketch",
     )(mine, other, ids)
 
 
-def solve(blocks, owners, query_ids):
+def solve(blocks, query_ids):
     count = len(blocks)
     size = count * E_DEV
     k_size = blocks[0].shape[0] * LANES // E_DEV
     queries = query_ids.shape[1]
 
     def kernel(*refs):
-        block_refs, owner_ref, ids_ref, out_ref = refs[:count], refs[count], refs[count + 1], refs[count + 2]
+        block_refs, ids_ref, out_ref = refs[:count], refs[count], refs[count + 1]
 
         def flat(ref):
             block = ref[...].astype(jnp.float32)
@@ -157,9 +165,11 @@
 
         spot = lax.broadcasted_iota(jnp.int32, (2 * size, queries), 0)
         place = (spot - size) // E_DEV
+        here, core = lax.axis_index("dp"), lax.axis_index("mp")
         example = jnp.full_like(spot, -1)
-        for b in range(count):
-            example = jnp.where(place == b, owner_ref[b] * E_DEV, example)
+        for b, pair in enumerate(ORDER):
+            owner = here ^ jnp.where(core == 0, pair[0], pair[1])
+            example = jnp.where(place == b, owner * E_DEV, example)
         example = example + spot % E_DEV
         chosen = jnp.where((spot >= size) & (example == ids_ref[...]), 1.0, 0.0).astype(jnp.bfloat16)
         high = result.astype(jnp.bfloat16)
@@ -173,10 +183,11 @@
     return pl.pallas_call(
         kernel,
         out_shape=jax.ShapeDtypeStruct((E_DEV, queries), jnp.float32),
-        in_specs=[vmem] * count + [pl.BlockSpec(memory_space=pltpu.SMEM), vmem],
+        in_specs=[vmem] * (count + 1),
         out_specs=vmem,
+        compiler_params=pltpu.CompilerParams(vmem_limit_bytes=8 * 2**20),
         name="solve",
-    )(*blocks, owners, query_ids)
+    )(*blocks, query_ids)
 
 
 def fetch(value, pair, count):
@@ -190,17 +201,13 @@
 
 def local_small(acts, out_grads, in_proj, out_proj, example_ids, query_ids):
     count = lax.axis_size("dp")
-    mine = project(acts, out_grads, in_proj.T, out_proj.T)
-    own = sketch(mine, swap(mine), example_ids, in_proj.shape[1])
+    mine, ids, queries = project(
+        acts, out_grads, in_proj.T, out_proj.T, example_ids, query_ids.reshape(1, -1)
+    )
+    own = sketch(mine, swap(mine), ids, in_proj.shape[1])
     near = [fetch(own, pair, count) for pair in STEPS]
     far = [swap(block) for block in near[1:]]
-    core = lax.axis_index("mp")
-    steps = jnp.array(
-        [[0] + [p[c] for p in STEPS] + [p[1 - c] for p in STEPS[1:]] for c in range(2)], jnp.int32
-    )
-    owners = steps[core] ^ lax.axis_index("dp")
-    picked = solve([own] + near + far, owners, query_ids.reshape(1, -1))
-    return picked.T
+    return solve([own] + near + far, queries).T
 
 
 def chol_solve(factor, rhs):

time: 26.2 us -> 18.4 us (0.70)
  local copies, waits for them, and re-layouts: 5.5 us -> 0 us
  Pallas kernels: 7.66 us -> 5.74 us
  waiting for transfers between devices: 1.13 us -> 1.7 us
  other arithmetic: 0.54 us -> 0 us
    unnamed x28 -> x0, local copies, waits for them, and re-layouts: 5.5 us -> none
    pallas_call x1, Pallas kernels: 1.54 us -> 0.16 us  [sketch(): pl.pallas_call(kernel, out_shape=jax.ShapeDtypeStruct((o_per * E_DEV, LAN...]
    pallas_call x1, Pallas kernels: 4.12 us -> 3.26 us  [solve(): pl.pallas_call(kernel, out_shape=jax.ShapeDtypeStruct((E_DEV, queries), j...]
    ppermute x4, waiting for transfers between devices: 1.12 us -> 1.69 us  [swap(): return lax.ppermute(value, 'mp', [(0, 1), (1, 0)])]
    xor x1 -> x0, other arithmetic: 0.54 us -> none  [local_small(): owners = steps[core] ^ lax.axis_index('dp')]
    pallas_call x1, Pallas kernels: 2 us -> 2.32 us  [project(): pl.pallas_call(kernel, out_shape=[jax.ShapeDtypeStruct((rin + rout, tok),...]
  transfers between devices with their start and end apart: 8 -> 8, of which waited for: 2 -> 2; matrix products, arithmetic and copies ran while one was open for 2% -> 0% of each run, Pallas kernels for 0% -> 0%
where the time goes in v2:
time: 18.4 us; the launch traced here: 18.3 us
  starting transfers between devices  10.8 us (59%)
  Pallas kernels  5.74 us (31%)
  waiting for transfers between devices  1.7 us (9%)
    ppermute x4, starting transfers between devices, fetch(): return lax.ppermute(value, ('dp', 'mp'), moves)  7.49 us
    ppermute x4, starting transfers between devices, swap(): return lax.ppermute(value, 'mp', [(0, 1), (1, 0)])  3.29 us
    pallas_call x1, Pallas kernels, solve(): pl.pallas_call(kernel, out_shape=jax.ShapeDtypeStruct((E_DEV, queries), j...  3.26 us
    pallas_call x1, Pallas kernels, project(): pl.pallas_call(kernel, out_shape=[jax.ShapeDtypeStruct((rin + rout, tok),...  2.32 us
    ppermute x4, waiting for transfers between devices, swap(): return lax.ppermute(value, 'mp', [(0, 1), (1, 0)])  1.69 us
  transfers between devices with their start and end apart: 8, of which 2 were waited for; matrix products, arithmetic and copies ran while one was open for 0% of the time, Pallas kernels for 0%

profile of v2, /device:TPU:0, one launch (start us, length us, event | category | flops | bytes accessed | tf_op | source)
XLA Modules:
  0.0 18.3 jit_solution(1995087433510452355)
XLA Ops:
  0.0 2.3 %project.1 = (f32[64,128]{1,0:T(8,128)S(1)}, s32[1,128]{1,0:T(1,128)S(1)}, s32[1,512]{1,0:T(1,128)S(1)}) custom-call(bf16[128,2048]{1,0:T(8,128)(2,1)} %a_hbm.1, bf16[128,5504]{1,0:T(8,128)(2,1)} %g_hbm.1, bf16[32,2048]{1,0:T(8,128)(2,1)} %bitcast.5, bf16[32,5504]{1,0:T(8,128)(2,1)} %bitcast.4, s32[1,128]{1,0:T(1,128)} %e_hbm.1, s32[1,512]{1,0:T(1,128)} %bitcast.6), custom_call_target="tpu_custom_call" | custom-call | tf_op jit(solution)/shard_map/project/pallas_call | solution.py:57
  2.3 0.5 %collective-permute-start = (f32[64,128]{1,0:T(8,128)S(1)}, f32[64,128]{1,0:T(8,128)S(1)}, u32[]{:S(2)}, u32[]{:S(2)}) collective-permute-start(f32[64,128]{1,0:T(8,128)S(1)} %get-tuple-element.8.mine_ref), channel_id=1, source_target_pairs={{0,1},{1,0},{2,3},{3,2},{4,5},{5,4},{6,7},{7,6},{8,9},{9,8},{10,11... | collective-permute-start | bytes 98312 | tf_op jit(solution)/shard_map/ppermute | solution.py:199
  2.9 0.9 %collective-permute-done.other_ref = f32[64,128]{1,0:T(8,128)S(1)} collective-permute-done((f32[64,128]{1,0:T(8,128)S(1)}, f32[64,128]{1,0:T(8,128)S(1)}, u32[]{:S(2)}, u32[]{:S(2)}) %collective-permute-start) | collective-permute-done | bytes 32800 | tf_op jit(solution)/shard_map/ppermute | solution.py:199
  3.7 0.2 sketch.1.refs_0_
  3.9 3.0 %collective-permute-start.4 = (bf16[64,128]{1,0:T(8,128)(2,1)S(1)}, bf16[64,128]{1,0:T(8,128)(2,1)S(1)}, u32[]{:S(2)}, u32[]{:S(2)}) collective-permute-start(bf16[64,128]{1,0:T(8,128)(2,1)S(1)} %sketch.1.refs_0_), channel_id=1, source_target_pairs={{0,4},{1,13},{2,6},{3,15},{4,0},{5,9},{6,2},{7,11},{8,12},{9,5},{1... | collective-permute-start | bytes 49160 | tf_op jit(solution)/shard_map/ppermute | solution.py:195
  6.9 1.5 %collective-permute-start.3 = (bf16[64,128]{1,0:T(8,128)(2,1)S(1)}, bf16[64,128]{1,0:T(8,128)(2,1)S(1)}, u32[]{:S(2)}, u32[]{:S(2)}) collective-permute-start(bf16[64,128]{1,0:T(8,128)(2,1)S(1)} %sketch.1.refs_0_), channel_id=1, source_target_pairs={{0,2},{1,11},{2,0},{3,9},{4,6},{5,15},{6,4},{7,13},{8,10},{9,3},{1... | collective-permute-start | bytes 49160 | tf_op jit(solution)/shard_map/ppermute | solution.py:195
  8.4 0.1 collective-permute-start.2
  8.4 3.0 %collective-permute-start.1 = (bf16[64,128]{1,0:T(8,128)(2,1)S(1)}, bf16[64,128]{1,0:T(8,128)(2,1)S(1)}, u32[]{:S(2)}, u32[]{:S(2)}) collective-permute-start(bf16[64,128]{1,0:T(8,128)(2,1)S(1)} %sketch.1.refs_0_), channel_id=1, source_target_pairs={{0,8},{1,9},{2,10},{3,11},{4,12},{5,13},{6,14},{7,15},{8,0},{9,1},... | collective-permute-start | bytes 49160 | tf_op jit(solution)/shard_map/ppermute | solution.py:195
  11.4 0.0 collective-permute-done.4.refs_4_
  11.4 0.7 %collective-permute-start.7 = (bf16[64,128]{1,0:T(8,128)(2,1)S(1)}, bf16[64,128]{1,0:T(8,128)(2,1)S(1)}, u32[]{:S(2)}, u32[]{:S(2)}) collective-permute-start(bf16[64,128]{1,0:T(8,128)(2,1)S(1)} %collective-permute-done.4.refs_4_), channel_id=1, source_target_pairs={{0,1},{1,0},{2,3},{3,2},{4,5},{5,4},{6,7},{7,6},{8,9},{9,8},{10,11... | collective-permute-start | bytes 49160 | tf_op jit(solution)/shard_map/ppermute | solution.py:199
  12.1 0.0 collective-permute-done.3.refs_3_
  12.1 1.1 %collective-permute-start.6 = (bf16[64,128]{1,0:T(8,128)(2,1)S(1)}, bf16[64,128]{1,0:T(8,128)(2,1)S(1)}, u32[]{:S(2)}, u32[]{:S(2)}) collective-permute-start(bf16[64,128]{1,0:T(8,128)(2,1)S(1)} %collective-permute-done.3.refs_3_), channel_id=1, source_target_pairs={{0,1},{1,0},{2,3},{3,2},{4,5},{5,4},{6,7},{7,6},{8,9},{9,8},{10,11... | collective-permute-start | bytes 49160 | tf_op jit(solution)/shard_map/ppermute | solution.py:199
  13.2 0.0 collective-permute-done.2.refs_2_
  13.2 1.0 %collective-permute-start.5 = (bf16[64,128]{1,0:T(8,128)(2,1)S(1)}, bf16[64,128]{1,0:T(8,128)(2,1)S(1)}, u32[]{:S(2)}, u32[]{:S(2)}) collective-permute-start(bf16[64,128]{1,0:T(8,128)(2,1)S(1)} %collective-permute-done.2.refs_2_), channel_id=1, source_target_pairs={{0,1},{1,0},{2,3},{3,2},{4,5},{5,4},{6,7},{7,6},{8,9},{9,8},{10,11... | collective-permute-start | bytes 49160 | tf_op jit(solution)/shard_map/ppermute | solution.py:199
  14.2 0.0 collective-permute-done.1.refs_1_
  14.2 0.0 collective-permute-done.7.refs_7_
  14.2 0.0 collective-permute-done.6.refs_6_
  14.2 0.8 %collective-permute-done.5.refs_5_ = bf16[64,128]{1,0:T(8,128)(2,1)S(1)} collective-permute-done((bf16[64,128]{1,0:T(8,128)(2,1)S(1)}, bf16[64,128]{1,0:T(8,128)(2,1)S(1)}, u32[]{:S(2)}, u32[]{:S(2)}) %collective-permute-start.5) | collective-permute-done | bytes 16416 | tf_op jit(solution)/shard_map/ppermute | solution.py:199
  15.0 3.3 %solve.1 = f32[8,512]{1,0:T(8,128)} custom-call(bf16[64,128]{1,0:T(8,128)(2,1)S(1)} %sketch.1.refs_0_, bf16[64,128]{1,0:T(8,128)(2,1)S(1)} %collective-permute-done.1.refs_1_, bf16[64,128]{1,0:T(8,128)(2,1)S(1)} %collective-permute-done.2.refs_2_, bf16[64,128]{1,0:T(8,128)(2,1)S(1)} %collective-permute-done.3.refs_3_, ...), custom_call_target="tpu_custom_call" | custom-call | tf_op jit(solution)/shard_map/solve/pallas_call | solution.py:183
Async XLA Ops:
  2.3 1.4 %collective-permute-start = (f32[64,128]{1,0:T(8,128)S(1)}, f32[64,128]{1,0:T(8,128)S(1)}, u32[]{:S(2)}, u32[]{:S(2)}) collective-permute-start(f32[64,128]{1,0:T(8,128)S(1)} %get-tuple-element.8.mine_ref), channel_id=1, source_target_pairs={{0,1},{1,0},{2,3},{3,2},{4,5},{5,4},{6,7},{7,6},{8,9},{9,8},{10,11... | collective-permute-start | bytes 98312 | tf_op jit(solution)/shard_map/ppermute | solution.py:199
  3.9 7.5 %collective-permute-start.4 = (bf16[64,128]{1,0:T(8,128)(2,1)S(1)}, bf16[64,128]{1,0:T(8,128)(2,1)S(1)}, u32[]{:S(2)}, u32[]{:S(2)}) collective-permute-start(bf16[64,128]{1,0:T(8,128)(2,1)S(1)} %sketch.1.refs_0_), channel_id=1, source_target_pairs={{0,4},{1,13},{2,6},{3,15},{4,0},{5,9},{6,2},{7,11},{8,12},{9,5},{1... | collective-permute-start | bytes 49160 | tf_op jit(solution)/shard_map/ppermute | solution.py:195
  6.9 5.2 %collective-permute-start.3 = (bf16[64,128]{1,0:T(8,128)(2,1)S(1)}, bf16[64,128]{1,0:T(8,128)(2,1)S(1)}, u32[]{:S(2)}, u32[]{:S(2)}) collective-permute-start(bf16[64,128]{1,0:T(8,128)(2,1)S(1)} %sketch.1.refs_0_), channel_id=1, source_target_pairs={{0,2},{1,11},{2,0},{3,9},{4,6},{5,15},{6,4},{7,13},{8,10},{9,3},{1... | collective-permute-start | bytes 49160 | tf_op jit(solution)/shard_map/ppermute | solution.py:195
  8.4 4.8 %collective-permute-start.2 = (bf16[64,128]{1,0:T(8,128)(2,1)S(1)}, bf16[64,128]{1,0:T(8,128)(2,1)S(1)}, u32[]{:S(2)}, u32[]{:S(2)}) collective-permute-start(bf16[64,128]{1,0:T(8,128)(2,1)S(1)} %sketch.1.refs_0_), channel_id=1, source_target_pairs={{0,6},{1,15},{2,4},{3,13},{4,2},{5,11},{6,0},{7,9},{8,14},{9,7},{1... | collective-permute-start | bytes 49160 | tf_op jit(solution)/shard_map/ppermute | solution.py:195
  8.4 5.8 %collective-permute-start.1 = (bf16[64,128]{1,0:T(8,128)(2,1)S(1)}, bf16[64,128]{1,0:T(8,128)(2,1)S(1)}, u32[]{:S(2)}, u32[]{:S(2)}) collective-permute-start(bf16[64,128]{1,0:T(8,128)(2,1)S(1)} %sketch.1.refs_0_), channel_id=1, source_target_pairs={{0,8},{1,9},{2,10},{3,11},{4,12},{5,13},{6,14},{7,15},{8,0},{9,1},... | collective-permute-start | bytes 49160 | tf_op jit(solution)/shard_map/ppermute | solution.py:195
  11.4 2.8 %collective-permute-start.7 = (bf16[64,128]{1,0:T(8,128)(2,1)S(1)}, bf16[64,128]{1,0:T(8,128)(2,1)S(1)}, u32[]{:S(2)}, u32[]{:S(2)}) collective-permute-start(bf16[64,128]{1,0:T(8,128)(2,1)S(1)} %collective-permute-done.4.refs_4_), channel_id=1, source_target_pairs={{0,1},{1,0},{2,3},{3,2},{4,5},{5,4},{6,7},{7,6},{8,9},{9,8},{10,11... | collective-permute-start | bytes 49160 | tf_op jit(solution)/shard_map/ppermute | solution.py:199
  12.1 2.1 %collective-permute-start.6 = (bf16[64,128]{1,0:T(8,128)(2,1)S(1)}, bf16[64,128]{1,0:T(8,128)(2,1)S(1)}, u32[]{:S(2)}, u32[]{:S(2)}) collective-permute-start(bf16[64,128]{1,0:T(8,128)(2,1)S(1)} %collective-permute-done.3.refs_3_), channel_id=1, source_target_pairs={{0,1},{1,0},{2,3},{3,2},{4,5},{5,4},{6,7},{7,6},{8,9},{9,8},{10,11... | collective-permute-start | bytes 49160 | tf_op jit(solution)/shard_map/ppermute | solution.py:199
  13.2 1.8 %collective-permute-start.5 = (bf16[64,128]{1,0:T(8,128)(2,1)S(1)}, bf16[64,128]{1,0:T(8,128)(2,1)S(1)}, u32[]{:S(2)}, u32[]{:S(2)}) collective-permute-start(bf16[64,128]{1,0:T(8,128)(2,1)S(1)} %collective-permute-done.2.refs_2_), channel_id=1, source_target_pairs={{0,1},{1,0},{2,3},{3,2},{4,5},{5,4},{6,7},{7,6},{8,9},{9,8},{10,11... | collective-permute-start | bytes 49160 | tf_op jit(solution)/shard_map/ppermute | solution.py:199

commit v3 on v2

--- a/solution.py
+++ b/solution.py
@@ -8,8 +8,19 @@
 E_DEV = 8
 LANES = 128
 NT = (((1,), (1,)), ((), ()))
-STEPS = ((4, 4), (3, 7), (1, 5), (2, 6))
-ORDER = ((0, 0),) + STEPS + tuple((b, a) for a, b in STEPS[1:])
+STEPS = (
+    ((5, 7, 0, 6, 2, 3, 4, 1), (5, 7, 0, 6, 2, 3, 4, 1)),
+    ((4, 0, 5, 1, 6, 2, 7, 3), (7, 5, 6, 0, 1, 4, 3, 2)),
+    ((2, 6, 3, 7, 0, 1, 5, 4), (6, 2, 7, 4, 3, 0, 1, 5)),
+    ((1, 3, 4, 2, 5, 7, 0, 6), (3, 4, 1, 5, 7, 6, 2, 0)),
+)
+
+
+def places(chip, core):
+    blocks = [chip]
+    blocks += [step[core].index(chip) for step in STEPS]
+    blocks += [step[1 - core].index(chip) for step in STEPS[1:]]
+    return sum(blocks.index(owner) << (4 * owner) for owner in range(len(blocks)))
 
 
 def chunks(size, parts):
@@ -18,12 +29,13 @@
     return [(s, min(per, size - s)) for s in starts]
 
 
-def project(acts, out_grads, in_t, out_t, example_ids, query_ids):
+def project(acts, out_grads, in_t, out_t, example_ids, query_ids, count):
     rin, rout = in_t.shape[0], out_t.shape[0]
     tok = acts.shape[0]
+    queries = query_ids.shape[1]
     g_cuts = chunks(out_grads.shape[1], 2)
 
-    def kernel(a_hbm, g_hbm, i_hbm, o_hbm, e_hbm, q_hbm, out_ref, e_ref, q_ref, a_v, g_v, i_v, o_v, sems):
+    def kernel(a_hbm, g_hbm, i_hbm, o_hbm, e_hbm, q_hbm, out_ref, e_ref, pick_ref, a_v, g_v, i_v, o_v, q_v, sems):
         copies = []
 
         def start(src, dst):
@@ -32,12 +44,22 @@
             copies.append(copy)
             return copy
 
+        q_copy = start(q_hbm, q_v)
         i_copy = start(i_hbm, i_v)
         a_copy = start(a_hbm, a_v)
         o_copy = start(o_hbm, o_v)
         g_copies = [start(g_hbm.at[:, pl.ds(s, n)], g_v.at[:, pl.ds(s, n)]) for s, n in g_cuts]
         e_copy = start(e_hbm, e_ref)
-        q_copy = start(q_hbm, q_ref)
+        q_copy.wait()
+        device = lax.axis_index("dp") * 2 + lax.axis_index("mp")
+        code = jnp.int32(0)
+        for n in range(2 * count):
+            bits = places(n // 2, n % 2)
+            code = jnp.where(device == n, bits - (bits >> 31 << 32), code)
+        ids = q_v[...]
+        spot = ((code >> (ids // E_DEV * 4)) & 7) * E_DEV + ids % E_DEV
+        row = lax.broadcasted_iota(jnp.int32, pick_ref.shape, 0)
+        pick_ref[...] = jnp.where(row == spot, 1.0, 0.0).astype(jnp.bfloat16)
         i_copy.wait()
         a_copy.wait()
         out_ref[0:rin, :] = lax.dot_general(i_v[...], a_v[...], NT, preferred_element_type=jnp.float32)
@@ -49,7 +71,6 @@
             total = term if total is None else total + term
         out_ref[rin : rin + rout, :] = total
         e_copy.wait()
-        q_copy.wait()
 
     hbm = pl.BlockSpec(memory_space=pltpu.HBM)
     vmem = pl.BlockSpec(memory_space=pltpu.VMEM)
@@ -59,7 +80,7 @@
         out_shape=[
             jax.ShapeDtypeStruct((rin + rout, tok), jnp.float32),
             jax.ShapeDtypeStruct(example_ids.shape, example_ids.dtype),
-            jax.ShapeDtypeStruct(query_ids.shape, query_ids.dtype),
+            jax.ShapeDtypeStruct((count * E_DEV, queries), jnp.bfloat16),
         ],
         in_specs=[hbm] * 6,
         out_specs=[vmem] * 3,
@@ -68,6 +89,7 @@
             pltpu.VMEM(out_grads.shape, out_grads.dtype),
             pltpu.VMEM(in_t.shape, in_t.dtype),
             pltpu.VMEM(out_t.shape, out_t.dtype),
+            pltpu.VMEM(query_ids.shape, query_ids.dtype),
             pltpu.SemaphoreType.DMA((5 + len(g_cuts),)),
         ],
         compiler_params=pltpu.CompilerParams(vmem_limit_bytes=16 * 2**20),
@@ -108,76 +130,85 @@
     )(mine, other, ids)
 
 
-def solve(blocks, query_ids):
+def solve(blocks, pick):
     count = len(blocks)
     size = count * E_DEV
     k_size = blocks[0].shape[0] * LANES // E_DEV
-    queries = query_ids.shape[1]
+    queries = pick.shape[1]
+    group = 2
 
     def kernel(*refs):
-        block_refs, ids_ref, out_ref = refs[:count], refs[count], refs[count + 1]
+        block_refs, pick_ref, out_ref = refs[:count], refs[count], refs[count + 1]
 
         def flat(ref):
             block = ref[...].astype(jnp.float32)
             cuts = [block[r : r + E_DEV] for r in range(0, block.shape[0], E_DEV)]
             return jnp.concatenate(cuts, axis=1)
 
-        every = jnp.concatenate([flat(ref) for ref in block_refs], axis=0).astype(jnp.bfloat16)
+        flats = [flat(ref) for ref in block_refs]
+        every = jnp.concatenate(flats, axis=0).astype(jnp.bfloat16)
         twice = jnp.concatenate([every, every], axis=0)
         gram = lax.dot_general(every, twice, NT, preferred_element_type=jnp.float32)
-        row = lax.broadcasted_iota(jnp.int32, (size, 2 * size), 0)
-        lane = lax.broadcasted_iota(jnp.int32, (size, 2 * size), 1)
-        diagonal = row == lane
-        damping = 0.1 * jnp.sum(jnp.where(diagonal, gram, 0.0)) / k_size
-        right_eye = jnp.where(row + size == lane, 1.0, 0.0)
-        system = jnp.where(lane < size, gram + jnp.where(diagonal, damping, 0.0), right_eye)
+        squares = sum(f * f for f in flats)
+        squares = sum(squares[:, s : s + LANES] for s in range(0, k_size, LANES))
+        total = jnp.sum(jnp.sum(squares, axis=0, keepdims=True), axis=1, keepdims=True)
+        shape = (E_DEV, 2 * size)
+        damping = jnp.broadcast_to(total * (0.1 / k_size), shape)
+        row = lax.broadcasted_iota(jnp.int32, gram.shape, 0)
+        lane = lax.broadcasted_iota(jnp.int32, gram.shape, 1)
+        system = jnp.where(lane < size, jnp.where(row == lane, 1.0, 0.0), gram)
         table = [system[r : r + E_DEV] for r in range(0, size, E_DEV)]
-        shape = table[0].shape
         sub = lax.broadcasted_iota(jnp.int32, shape, 0)
+        lane = lax.broadcasted_iota(jnp.int32, shape, 1)
+        here = [sub == i for i in range(E_DEV)]
 
         def down(value, i):
             return jnp.broadcast_to(value[i : i + 1], shape)
 
-        for k in range(count):
-            wide = [[jnp.broadcast_to(t[:, c : c + 1], shape) for c in range(k * E_DEV, (k + 1) * E_DEV)] for t in table]
-            pivot, cols = table[k], wide[k]
-            for i in range(E_DEV):
-                scale = 1.0 / down(cols[i], i)
-                here = sub == i
-                factor = cols[i]
-
-                def clear(value):
-                    line = down(value, i) * scale
-                    return jnp.where(here, line, value - factor * line)
-
-                pivot = clear(pivot)
-                cols = [clear(c) if j > i else c for j, c in enumerate(cols)]
-            table[k] = pivot
-            lines = [down(pivot, j) for j in range(E_DEV)]
+        for first in range(0, count, group):
+            own = range(group)
+            base = size + first * E_DEV
+            wide = [[jnp.broadcast_to(t[:, c : c + 1], shape) for c in range(base, base + group * E_DEV)] for t in table]
+            rows = [
+                table[first + k] + jnp.where(lane == sub + (base + k * E_DEV), damping, 0.0) for k in own
+            ]
+            cols = [
+                [wide[first + k][j] + jnp.where(here[j % E_DEV], damping, 0.0) if j // E_DEV == k else wide[first + k][j]
+                 for j in range(group * E_DEV)]
+                for k in own
+            ]
+            scales = [jnp.zeros(shape, jnp.float32) for k in own]
+            for i in range(group * E_DEV):
+                which, at = i // E_DEV, i % E_DEV
+                scale = 1.0 / down(cols[which][i], at)
+                scales[which] = jnp.where(here[at], scale, scales[which])
+                factor = [jnp.where(here[at], 0.0, cols[k][i]) if k == which else cols[k][i] for k in own]
+
+                def clear(values):
+                    line = down(values[which], at)
+                    return [values[k] - (factor[k] * line) * scale for k in own]
+
+                for j in range(i + 1, group * E_DEV):
+                    fresh = clear([cols[k][j] for k in own])
+                    for k in own:
+                        cols[k][j] = fresh[k]
+                rows = clear(rows)
+            for k in own:
+                table[first + k] = rows[k] * scales[k]
+            lines = [down(table[first + j // E_DEV], j % E_DEV) for j in range(group * E_DEV)]
             for r in range(count):
-                if r != k:
-                    drop = wide[r][0] * lines[0]
-                    for j in range(1, E_DEV):
-                        drop = drop + wide[r][j] * lines[j]
-                    table[r] = table[r] - drop
-        eye = jnp.where(sub + size == lane[0:E_DEV], 1.0, 0.0)
-        result = jnp.where(lane[0:E_DEV] >= size, eye - damping * table[0], 0.0)
-
-        spot = lax.broadcasted_iota(jnp.int32, (2 * size, queries), 0)
-        place = (spot - size) // E_DEV
-        here, core = lax.axis_index("dp"), lax.axis_index("mp")
-        example = jnp.full_like(spot, -1)
-        for b, pair in enumerate(ORDER):
-            owner = here ^ jnp.where(core == 0, pair[0], pair[1])
-            example = jnp.where(place == b, owner * E_DEV, example)
-        example = example + spot % E_DEV
-        chosen = jnp.where((spot >= size) & (example == ids_ref[...]), 1.0, 0.0).astype(jnp.bfloat16)
-        high = result.astype(jnp.bfloat16)
-        rest = result - high.astype(jnp.float32)
-        mid = rest.astype(jnp.bfloat16)
-        low = (rest - mid.astype(jnp.float32)).astype(jnp.bfloat16)
-        picks = [jnp.dot(part, chosen, preferred_element_type=jnp.float32) for part in (high, mid, low)]
-        out_ref[...] = picks[0] + (picks[1] + picks[2])
+                if not first <= r < first + group:
+                    terms = [wide[r][j] * lines[j] for j in range(group * E_DEV)]
+                    while len(terms) > 1:
+                        terms = [x + y for x, y in zip(terms[::2], terms[1::2])]
+                    table[r] = table[r] - terms[0]
+
+        result = (jnp.where(sub == lane, 1.0, 0.0) - damping * table[0])[:, 0:size]
+        high = result.astype(jnp.bfloat16).astype(jnp.float32)
+        mid = (result - high).astype(jnp.bfloat16).astype(jnp.float32)
+        parts = jnp.concatenate([high, mid, result - high - mid], axis=0).astype(jnp.bfloat16)
+        rows = jnp.dot(parts, pick_ref[...], preferred_element_type=jnp.float32)
+        out_ref[...] = rows[0:E_DEV] + (rows[E_DEV : 2 * E_DEV] + rows[2 * E_DEV : 3 * E_DEV])
 
     vmem = pl.BlockSpec(memory_space=pltpu.VMEM)
     return pl.pallas_call(
@@ -187,11 +218,11 @@
         out_specs=vmem,
         compiler_params=pltpu.CompilerParams(vmem_limit_bytes=8 * 2**20),
         name="solve",
-    )(*blocks, query_ids)
-
-
-def fetch(value, pair, count):
-    moves = [(2 * i + c, 2 * (i ^ pair[c]) + c) for i in range(count) for c in range(2)]
+    )(*blocks, pick)
+
+
+def fetch(value, step):
+    moves = [(2 * i + c, 2 * to + c) for c in range(2) for i, to in enumerate(step[c])]
     return lax.ppermute(value, ("dp", "mp"), moves)
 
 
@@ -201,13 +232,13 @@
 
 def local_small(acts, out_grads, in_proj, out_proj, example_ids, query_ids):
     count = lax.axis_size("dp")
-    mine, ids, queries = project(
-        acts, out_grads, in_proj.T, out_proj.T, example_ids, query_ids.reshape(1, -1)
+    mine, ids, pick = project(
+        acts, out_grads, in_proj.T, out_proj.T, example_ids, query_ids.reshape(1, -1), count
     )
     own = sketch(mine, swap(mine), ids, in_proj.shape[1])
-    near = [fetch(own, pair, count) for pair in STEPS]
+    near = [fetch(own, step) for step in STEPS]
     far = [swap(block) for block in near[1:]]
-    return solve([own] + near + far, queries).T
+    return solve([own] + near + far, pick).T
 
 
 def chol_solve(factor, rhs):

time: 18.4 us -> 16.2 us (0.88)
  the two profiles are of different devices: /device:TPU:0 before, /device:TPU:7 now
where the time goes in v3:
time: 16.2 us; the launch traced here: 16 us
  starting transfers between devices  8.71 us (54%)
  Pallas kernels  4.98 us (31%)
  waiting for transfers between devices  2.31 us (14%)
    ppermute x4, starting transfers between devices, fetch(): return lax.ppermute(value, ('dp', 'mp'), moves)  6.7 us
    pallas_call x1, Pallas kernels, solve(): pl.pallas_call(kernel, out_shape=jax.ShapeDtypeStruct((E_DEV, queries), j...  2.49 us
    pallas_call x1, Pallas kernels, project(): pl.pallas_call(kernel, out_shape=[jax.ShapeDtypeStruct((rin + rout, tok),...  2.34 us
    ppermute x4, starting transfers between devices, swap(): return lax.ppermute(value, 'mp', [(0, 1), (1, 0)])  2.01 us
    ppermute x4, waiting for transfers between devices, fetch(): return lax.ppermute(value, ('dp', 'mp'), moves)  1.45 us
    ppermute x4, waiting for transfers between devices, swap(): return lax.ppermute(value, 'mp', [(0, 1), (1, 0)])  0.87 us
  transfers between devices with their start and end apart: 8, of which 3 were waited for; matrix products, arithmetic and copies ran while one was open for 0% of the time, Pallas kernels for 0%

profile of v3, /device:TPU:7, one launch (start us, length us, event | category | flops | bytes accessed | tf_op | source)
XLA Modules:
  0.0 16.0 jit_solution(5271398784622864722)
XLA Ops:
  0.0 2.3 %project.1 = (f32[64,128]{1,0:T(8,128)S(1)}, s32[1,128]{1,0:T(1,128)S(1)}, bf16[64,512]{1,0:T(8,128)(2,1)S(1)}) custom-call(bf16[128,2048]{1,0:T(8,128)(2,1)} %a_hbm.1, bf16[128,5504]{1,0:T(8,128)(2,1)} %g_hbm.1, bf16[32,2048]{1,0:T(8,128)(2,1)} %bitcast.5, bf16[32,5504]{1,0:T(8,128)(2,1)} %bitcast.4, s32[1,128]{1,0:T(1,128)} %e_hbm.1, s32[1,512]{1,0:T(1,128)} %bitcast.6), custom_call_target="tpu_custom_call" | custom-call | tf_op jit(solution)/shard_map/project/pallas_call | solution.py:78
  2.3 0.7 %collective-permute-start = (f32[64,128]{1,0:T(8,128)S(1)}, f32[64,128]{1,0:T(8,128)S(1)}, u32[]{:S(2)}, u32[]{:S(2)}) collective-permute-start(f32[64,128]{1,0:T(8,128)S(1)} %get-tuple-element.8.mine_ref), channel_id=1, source_target_pairs={{0,1},{1,0},{2,3},{3,2},{4,5},{5,4},{6,7},{7,6},{8,9},{9,8},{10,11... | collective-permute-start | bytes 98312 | tf_op jit(solution)/shard_map/ppermute | solution.py:230
  3.1 0.9 %collective-permute-done.other_ref = f32[64,128]{1,0:T(8,128)S(1)} collective-permute-done((f32[64,128]{1,0:T(8,128)S(1)}, f32[64,128]{1,0:T(8,128)S(1)}, u32[]{:S(2)}, u32[]{:S(2)}) %collective-permute-start) | collective-permute-done | bytes 32800 | tf_op jit(solution)/shard_map/ppermute | solution.py:230
  3.9 0.2 sketch.1.refs_0_
  4.1 2.3 %collective-permute-start.4 = (bf16[64,128]{1,0:T(8,128)(2,1)S(1)}, bf16[64,128]{1,0:T(8,128)(2,1)S(1)}, u32[]{:S(2)}, u32[]{:S(2)}) collective-permute-start(bf16[64,128]{1,0:T(8,128)(2,1)S(1)} %sketch.1.refs_0_), channel_id=1, source_target_pairs={{0,2},{2,6},{4,8},{6,4},{8,10},{10,14},{12,0},{14,12},{1,7},{3,9},... | collective-permute-start | bytes 49160 | tf_op jit(solution)/shard_map/ppermute | solution.py:226
  6.4 0.1 collective-permute-start.3
  6.5 2.2 %collective-permute-start.2 = (bf16[64,128]{1,0:T(8,128)(2,1)S(1)}, bf16[64,128]{1,0:T(8,128)(2,1)S(1)}, u32[]{:S(2)}, u32[]{:S(2)}) collective-permute-start(bf16[64,128]{1,0:T(8,128)(2,1)S(1)} %sketch.1.refs_0_), channel_id=1, source_target_pairs={{0,8},{2,0},{4,10},{6,2},{8,12},{10,4},{12,14},{14,6},{1,15},{3,11... | collective-permute-start | bytes 49160 | tf_op jit(solution)/shard_map/ppermute | solution.py:226
  8.7 2.1 %collective-permute-start.1 = (bf16[64,128]{1,0:T(8,128)(2,1)S(1)}, bf16[64,128]{1,0:T(8,128)(2,1)S(1)}, u32[]{:S(2)}, u32[]{:S(2)}) collective-permute-start(bf16[64,128]{1,0:T(8,128)(2,1)S(1)} %sketch.1.refs_0_), channel_id=1, source_target_pairs={{0,10},{2,14},{4,0},{6,12},{8,4},{10,6},{12,8},{14,2},{1,11},{3,15... | collective-permute-start | bytes 49160 | tf_op jit(solution)/shard_map/ppermute | solution.py:226
  10.8 0.0 collective-permute-done.4.refs_4_
  10.8 0.8 %collective-permute-start.7 = (bf16[64,128]{1,0:T(8,128)(2,1)S(1)}, bf16[64,128]{1,0:T(8,128)(2,1)S(1)}, u32[]{:S(2)}, u32[]{:S(2)}) collective-permute-start(bf16[64,128]{1,0:T(8,128)(2,1)S(1)} %collective-permute-done.4.refs_4_), channel_id=1, source_target_pairs={{0,1},{1,0},{2,3},{3,2},{4,5},{5,4},{6,7},{7,6},{8,9},{9,8},{10,11... | collective-permute-start | bytes 49160 | tf_op jit(solution)/shard_map/ppermute | solution.py:230
  11.6 0.2 collective-permute-done.3.refs_3_
  11.7 0.0 collective-permute-start.6
  11.7 0.0 collective-permute-done.2.refs_2_
  11.7 0.5 %collective-permute-start.5 = (bf16[64,128]{1,0:T(8,128)(2,1)S(1)}, bf16[64,128]{1,0:T(8,128)(2,1)S(1)}, u32[]{:S(2)}, u32[]{:S(2)}) collective-permute-start(bf16[64,128]{1,0:T(8,128)(2,1)S(1)} %collective-permute-done.2.refs_2_), channel_id=1, source_target_pairs={{0,1},{1,0},{2,3},{3,2},{4,5},{5,4},{6,7},{7,6},{8,9},{9,8},{10,11... | collective-permute-start | bytes 49160 | tf_op jit(solution)/shard_map/ppermute | solution.py:230
  12.2 1.3 %collective-permute-done.1.refs_1_ = bf16[64,128]{1,0:T(8,128)(2,1)S(1)} collective-permute-done((bf16[64,128]{1,0:T(8,128)(2,1)S(1)}, bf16[64,128]{1,0:T(8,128)(2,1)S(1)}, u32[]{:S(2)}, u32[]{:S(2)}) %collective-permute-start.1) | collective-permute-done | bytes 16416 | tf_op jit(solution)/shard_map/ppermute | solution.py:226
  13.5 0.0 collective-permute-done.7.refs_7_
  13.5 0.0 collective-permute-done.6.refs_6_
  13.5 0.0 collective-permute-done.5.refs_5_
  13.5 2.5 %solve.1 = f32[8,512]{1,0:T(8,128)} custom-call(bf16[64,128]{1,0:T(8,128)(2,1)S(1)} %sketch.1.refs_0_, bf16[64,128]{1,0:T(8,128)(2,1)S(1)} %collective-permute-done.1.refs_1_, bf16[64,128]{1,0:T(8,128)(2,1)S(1)} %collective-permute-done.2.refs_2_, bf16[64,128]{1,0:T(8,128)(2,1)S(1)} %collective-permute-done.3.refs_3_, ...), custom_call_target="tpu_custom_call" | custom-call | tf_op jit(solution)/shard_map/solve/pallas_call | solution.py:214
Async XLA Ops:
  2.3 1.6 %collective-permute-start = (f32[64,128]{1,0:T(8,128)S(1)}, f32[64,128]{1,0:T(8,128)S(1)}, u32[]{:S(2)}, u32[]{:S(2)}) collective-permute-start(f32[64,128]{1,0:T(8,128)S(1)} %get-tuple-element.8.mine_ref), channel_id=1, source_target_pairs={{0,1},{1,0},{2,3},{3,2},{4,5},{5,4},{6,7},{7,6},{8,9},{9,8},{10,11... | collective-permute-start | bytes 98312 | tf_op jit(solution)/shard_map/ppermute | solution.py:230
  4.1 6.7 %collective-permute-start.4 = (bf16[64,128]{1,0:T(8,128)(2,1)S(1)}, bf16[64,128]{1,0:T(8,128)(2,1)S(1)}, u32[]{:S(2)}, u32[]{:S(2)}) collective-permute-start(bf16[64,128]{1,0:T(8,128)(2,1)S(1)} %sketch.1.refs_0_), channel_id=1, source_target_pairs={{0,2},{2,6},{4,8},{6,4},{8,10},{10,14},{12,0},{14,12},{1,7},{3,9},... | collective-permute-start | bytes 49160 | tf_op jit(solution)/shard_map/ppermute | solution.py:226
  6.4 5.3 %collective-permute-start.3 = (bf16[64,128]{1,0:T(8,128)(2,1)S(1)}, bf16[64,128]{1,0:T(8,128)(2,1)S(1)}, u32[]{:S(2)}, u32[]{:S(2)}) collective-permute-start(bf16[64,128]{1,0:T(8,128)(2,1)S(1)} %sketch.1.refs_0_), channel_id=1, source_target_pairs={{0,4},{2,12},{4,6},{6,14},{8,0},{10,2},{12,10},{14,8},{1,13},{3,5}... | collective-permute-start | bytes 49160 | tf_op jit(solution)/shard_map/ppermute | solution.py:226
  6.5 5.2 %collective-permute-start.2 = (bf16[64,128]{1,0:T(8,128)(2,1)S(1)}, bf16[64,128]{1,0:T(8,128)(2,1)S(1)}, u32[]{:S(2)}, u32[]{:S(2)}) collective-permute-start(bf16[64,128]{1,0:T(8,128)(2,1)S(1)} %sketch.1.refs_0_), channel_id=1, source_target_pairs={{0,8},{2,0},{4,10},{6,2},{8,12},{10,4},{12,14},{14,6},{1,15},{3,11... | collective-permute-start | bytes 49160 | tf_op jit(solution)/shard_map/ppermute | solution.py:226
  8.7 4.8 %collective-permute-start.1 = (bf16[64,128]{1,0:T(8,128)(2,1)S(1)}, bf16[64,128]{1,0:T(8,128)(2,1)S(1)}, u32[]{:S(2)}, u32[]{:S(2)}) collective-permute-start(bf16[64,128]{1,0:T(8,128)(2,1)S(1)} %sketch.1.refs_0_), channel_id=1, source_target_pairs={{0,10},{2,14},{4,0},{6,12},{8,4},{10,6},{12,8},{14,2},{1,11},{3,15... | collective-permute-start | bytes 49160 | tf_op jit(solution)/shard_map/ppermute | solution.py:226
  10.8 2.7 %collective-permute-start.7 = (bf16[64,128]{1,0:T(8,128)(2,1)S(1)}, bf16[64,128]{1,0:T(8,128)(2,1)S(1)}, u32[]{:S(2)}, u32[]{:S(2)}) collective-permute-start(bf16[64,128]{1,0:T(8,128)(2,1)S(1)} %collective-permute-done.4.refs_4_), channel_id=1, source_target_pairs={{0,1},{1,0},{2,3},{3,2},{4,5},{5,4},{6,7},{7,6},{8,9},{9,8},{10,11... | collective-permute-start | bytes 49160 | tf_op jit(solution)/shard_map/ppermute | solution.py:230
  11.7 1.8 %collective-permute-start.6 = (bf16[64,128]{1,0:T(8,128)(2,1)S(1)}, bf16[64,128]{1,0:T(8,128)(2,1)S(1)}, u32[]{:S(2)}, u32[]{:S(2)}) collective-permute-start(bf16[64,128]{1,0:T(8,128)(2,1)S(1)} %collective-permute-done.3.refs_3_), channel_id=1, source_target_pairs={{0,1},{1,0},{2,3},{3,2},{4,5},{5,4},{6,7},{7,6},{8,9},{9,8},{10,11... | collective-permute-start | bytes 49160 | tf_op jit(solution)/shard_map/ppermute | solution.py:230
  11.7 1.8 %collective-permute-start.5 = (bf16[64,128]{1,0:T(8,128)(2,1)S(1)}, bf16[64,128]{1,0:T(8,128)(2,1)S(1)}, u32[]{:S(2)}, u32[]{:S(2)}) collective-permute-start(bf16[64,128]{1,0:T(8,128)(2,1)S(1)} %collective-permute-done.2.refs_2_), channel_id=1, source_target_pairs={{0,1},{1,0},{2,3},{3,2},{4,5},{5,4},{6,7},{7,6},{8,9},{9,8},{10,11... | collective-permute-start | bytes 49160 | tf_op jit(solution)/shard_map/ppermute | solution.py:230

commit v4 on v3

--- a/solution.py
+++ b/solution.py
@@ -9,17 +9,17 @@
 LANES = 128
 NT = (((1,), (1,)), ((), ()))
 STEPS = (
-    ((5, 7, 0, 6, 2, 3, 4, 1), (5, 7, 0, 6, 2, 3, 4, 1)),
-    ((4, 0, 5, 1, 6, 2, 7, 3), (7, 5, 6, 0, 1, 4, 3, 2)),
-    ((2, 6, 3, 7, 0, 1, 5, 4), (6, 2, 7, 4, 3, 0, 1, 5)),
-    ((1, 3, 4, 2, 5, 7, 0, 6), (3, 4, 1, 5, 7, 6, 2, 0)),
+    (7, 6, 1, 0, 3, 2, 8, 9, 15, 14, 13, 12, 10, 11, 5, 4),
+    (11, 15, 13, 4, 9, 1, 10, 0, 3, 7, 14, 2, 5, 6, 12, 8),
+    (9, 13, 15, 10, 14, 6, 2, 4, 12, 5, 8, 1, 3, 0, 7, 11),
+    (5, 3, 9, 6, 13, 10, 15, 12, 11, 0, 4, 7, 14, 8, 1, 2),
 )
 
 
-def places(chip, core):
-    blocks = [chip]
-    blocks += [step[core].index(chip) for step in STEPS]
-    blocks += [step[1 - core].index(chip) for step in STEPS[1:]]
+def places(device):
+    blocks = [device // 2]
+    blocks += [step.index(device) // 2 for step in STEPS]
+    blocks += [step.index(device ^ 1) // 2 for step in STEPS[1:]]
     return sum(blocks.index(owner) << (4 * owner) for owner in range(len(blocks)))
 
 
@@ -54,7 +54,7 @@
         device = lax.axis_index("dp") * 2 + lax.axis_index("mp")
         code = jnp.int32(0)
         for n in range(2 * count):
-            bits = places(n // 2, n % 2)
+            bits = places(n)
             code = jnp.where(device == n, bits - (bits >> 31 << 32), code)
         ids = q_v[...]
         spot = ((code >> (ids // E_DEV * 4)) & 7) * E_DEV + ids % E_DEV
@@ -136,9 +136,10 @@
     k_size = blocks[0].shape[0] * LANES // E_DEV
     queries = pick.shape[1]
     group = 2
+    span = group * E_DEV
 
     def kernel(*refs):
-        block_refs, pick_ref, out_ref = refs[:count], refs[count], refs[count + 1]
+        block_refs, pick_ref, out_ref, basis = refs[:count], refs[count], refs[count + 1], refs[count + 2]
 
         def flat(ref):
             block = ref[...].astype(jnp.float32)
@@ -156,11 +157,15 @@
         damping = jnp.broadcast_to(total * (0.1 / k_size), shape)
         row = lax.broadcasted_iota(jnp.int32, gram.shape, 0)
         lane = lax.broadcasted_iota(jnp.int32, gram.shape, 1)
-        system = jnp.where(lane < size, jnp.where(row == lane, 1.0, 0.0), gram)
+        diagonal = row == lane
+        system = jnp.where(lane < size, jnp.where(diagonal, 1.0, 0.0), gram)
         table = [system[r : r + E_DEV] for r in range(0, size, E_DEV)]
         sub = lax.broadcasted_iota(jnp.int32, shape, 0)
         lane = lax.broadcasted_iota(jnp.int32, shape, 1)
         here = [sub == i for i in range(E_DEV)]
+        norms = jnp.sum(jnp.where(diagonal, gram, 0.0), axis=1, keepdims=True)
+        norms = [jnp.broadcast_to(norms[r : r + E_DEV], shape) for r in range(0, size, E_DEV)]
+        spread = jnp.zeros(shape, jnp.float32)
 
         def down(value, i):
             return jnp.broadcast_to(value[i : i + 1], shape)
@@ -168,47 +173,89 @@
         for first in range(0, count, group):
             own = range(group)
             base = size + first * E_DEV
-            wide = [[jnp.broadcast_to(t[:, c : c + 1], shape) for c in range(base, base + group * E_DEV)] for t in table]
-            rows = [
-                table[first + k] + jnp.where(lane == sub + (base + k * E_DEV), damping, 0.0) for k in own
-            ]
-            cols = [
-                [wide[first + k][j] + jnp.where(here[j % E_DEV], damping, 0.0) if j // E_DEV == k else wide[first + k][j]
-                 for j in range(group * E_DEV)]
-                for k in own
-            ]
-            scales = [jnp.zeros(shape, jnp.float32) for k in own]
-            for i in range(group * E_DEV):
+            wide = [[jnp.broadcast_to(t[:, c : c + 1], shape) for c in range(base, base + span)] for t in table]
+            rows = [table[first + k] + jnp.where(lane == sub + (base + k * E_DEV), damping, 0.0) for k in own]
+            cols = [list(wide[first + k]) for k in own]
+            for j in range(span):
+                k = j // E_DEV
+                cols[k][j] = cols[k][j] + jnp.where(here[j % E_DEV], damping, 0.0)
+            scalings = []
+            for i in range(0, span, 2):
                 which, at = i // E_DEV, i % E_DEV
-                scale = 1.0 / down(cols[which][i], at)
-                scales[which] = jnp.where(here[at], scale, scales[which])
-                factor = [jnp.where(here[at], 0.0, cols[k][i]) if k == which else cols[k][i] for k in own]
+                p, q = down(cols[which][i], at), down(cols[which][i + 1], at)
+                s, t = down(cols[which][i], at + 1), down(cols[which][i + 1], at + 1)
+                inverse = 1.0 / (p * t - q * s)
+                scalings.append((t * inverse, q * inverse, p * inverse, s * inverse))
+                norm = norms[first + which]
+                spread = spread + (down(norm, at) * scalings[-1][0] + down(norm, at + 1) * scalings[-1][2])
+                factors = []
+                for k in own:
+                    x, y = cols[k][i], cols[k][i + 1]
+                    pair = (x * t - y * s, y * p - x * q)
+                    if k == which:
+                        pair = [jnp.where(here[at] | here[at + 1], 0.0, f) for f in pair]
+                    factors.append([f * inverse for f in pair])
 
                 def clear(values):
-                    line = down(values[which], at)
-                    return [values[k] - (factor[k] * line) * scale for k in own]
-
-                for j in range(i + 1, group * E_DEV):
+                    upper, lower = down(values[which], at), down(values[which], at + 1)
+                    return [values[k] - (factors[k][0] * upper + factors[k][1] * lower) for k in own]
+
+                for j in range(i + 2, span):
                     fresh = clear([cols[k][j] for k in own])
                     for k in own:
                         cols[k][j] = fresh[k]
                 rows = clear(rows)
             for k in own:
-                table[first + k] = rows[k] * scales[k]
-            lines = [down(table[first + j // E_DEV], j % E_DEV) for j in range(group * E_DEV)]
+                scaled = rows[k]
+                for at in range(0, E_DEV, 2):
+                    a, b, c, d = scalings[(k * E_DEV + at) // 2]
+                    upper, lower = down(rows[k], at), down(rows[k], at + 1)
+                    scaled = jnp.where(here[at], a * upper - b * lower, scaled)
+                    scaled = jnp.where(here[at + 1], c * lower - d * upper, scaled)
+                table[first + k] = scaled
+            lines = [down(table[first + j // E_DEV], j % E_DEV) for j in range(span)]
             for r in range(count):
                 if not first <= r < first + group:
-                    terms = [wide[r][j] * lines[j] for j in range(group * E_DEV)]
+                    terms = [wide[r][j] * lines[j] for j in range(span)]
                     while len(terms) > 1:
                         terms = [x + y for x, y in zip(terms[::2], terms[1::2])]
                     table[r] = table[r] - terms[0]
 
-        result = (jnp.where(sub == lane, 1.0, 0.0) - damping * table[0])[:, 0:size]
-        high = result.astype(jnp.bfloat16).astype(jnp.float32)
-        mid = (result - high).astype(jnp.bfloat16).astype(jnp.float32)
-        parts = jnp.concatenate([high, mid, result - high - mid], axis=0).astype(jnp.bfloat16)
-        rows = jnp.dot(parts, pick_ref[...], preferred_element_type=jnp.float32)
-        out_ref[...] = rows[0:E_DEV] + (rows[E_DEV : 2 * E_DEV] + rows[2 * E_DEV : 3 * E_DEV])
+        eye = jnp.where(sub == lane, 1.0, 0.0)
+
+        def picked(result):
+            result = result[:, 0:size]
+            high = result.astype(jnp.bfloat16).astype(jnp.float32)
+            mid = (result - high).astype(jnp.bfloat16).astype(jnp.float32)
+            parts = jnp.concatenate([high, mid, result - high - mid], axis=0).astype(jnp.bfloat16)
+            found = jnp.dot(parts, pick_ref[...], preferred_element_type=jnp.float32)
+            return found[0:E_DEV] + (found[E_DEV : 2 * E_DEV] + found[2 * E_DEV : 3 * E_DEV])
+
+        out_ref[...] = picked(eye - damping * table[0])
+
+        @pl.when(spread[0, 0] > 4.0 * size)
+        def _():
+            for k, ref in enumerate(block_refs):
+                basis[k * E_DEV : (k + 1) * E_DEV, 0:k_size] = flat(ref)
+            root = jnp.sqrt(damping[0:1, :])
+            basis[:, k_size : k_size + 2 * size] = jnp.where(diagonal, jnp.broadcast_to(root, gram.shape), 0.0)
+            number = lax.broadcasted_iota(jnp.int32, (size, 1), 0)
+
+            def step(i, carry):
+                line = basis[pl.ds(i, 1), :]
+                line = line / jnp.sqrt(jnp.sum(line * line, axis=1, keepdims=True))
+                everything = basis[...]
+                part = jnp.sum(everything * line, axis=1, keepdims=True)
+                part = jnp.where(number > i, part, 0.0)
+                basis[...] = jnp.where(number == i, line, everything - part * line)
+                return carry
+
+            lax.fori_loop(0, size, step, 0)
+            tail = basis[:, k_size : k_size + 2 * size]
+            rest = lax.dot_general(
+                tail, tail, (((0,), (0,)), ((), ())), precision=lax.Precision.HIGHEST, preferred_element_type=jnp.float32
+            )
+            out_ref[...] = picked(eye - rest[0:E_DEV])
 
     vmem = pl.BlockSpec(memory_space=pltpu.VMEM)
     return pl.pallas_call(
@@ -216,14 +263,14 @@
         out_shape=jax.ShapeDtypeStruct((E_DEV, queries), jnp.float32),
         in_specs=[vmem] * (count + 1),
         out_specs=vmem,
+        scratch_shapes=[pltpu.VMEM((size, k_size + 2 * size), jnp.float32)],
         compiler_params=pltpu.CompilerParams(vmem_limit_bytes=8 * 2**20),
         name="solve",
     )(*blocks, pick)
 
 
 def fetch(value, step):
-    moves = [(2 * i + c, 2 * to + c) for c in range(2) for i, to in enumerate(step[c])]
-    return lax.ppermute(value, ("dp", "mp"), moves)
+    return lax.ppermute(value, ("dp", "mp"), list(enumerate(step)))
 
 
 def swap(value):

time: 16.2 us -> 15.8 us (0.975)
  starting transfers between devices: 8.71 us -> 6.2 us
  waiting for transfers between devices: 2.31 us -> 4.62 us
  Pallas kernels: 4.98 us -> 4.74 us
    ppermute x4, waiting for transfers between devices: 1.45 us -> 3.75 us  [fetch(): return lax.ppermute(value, ('dp', 'mp'), list(enumerate(step)))]
    ppermute x4, starting transfers between devices: 6.7 us -> 5.15 us  [fetch(): return lax.ppermute(value, ('dp', 'mp'), list(enumerate(step)))]
    ppermute x4, starting transfers between devices: 2.01 us -> 1.05 us  [swap(): return lax.ppermute(value, 'mp', [(0, 1), (1, 0)])]
    pallas_call x1, Pallas kernels: 2.49 us -> 2.25 us  [solve(): pl.pallas_call(kernel, out_shape=jax.ShapeDtypeStruct((E_DEV, queries), j...]
  transfers between devices with their start and end apart: 8 -> 8, of which waited for: 3 -> 4; matrix products, arithmetic and copies ran while one was open for 0% -> 0% of each run, Pallas kernels for 0% -> 0%
where the time goes in v4:
time: 15.8 us; the launch traced here: 15.6 us
  starting transfers between devices  6.2 us (39%)
  Pallas kernels  4.74 us (30%)
  waiting for transfers between devices  4.62 us (29%)
    ppermute x4, starting transfers between devices, fetch(): return lax.ppermute(value, ('dp', 'mp'), list(enumerate(step)))  5.15 us
    ppermute x4, waiting for transfers between devices, fetch(): return lax.ppermute(value, ('dp', 'mp'), list(enumerate(step)))  3.75 us
    pallas_call x1, Pallas kernels, project(): pl.pallas_call(kernel, out_shape=[jax.ShapeDtypeStruct((rin + rout, tok),...  2.34 us
    pallas_call x1, Pallas kernels, solve(): pl.pallas_call(kernel, out_shape=jax.ShapeDtypeStruct((E_DEV, queries), j...  2.25 us
    ppermute x4, starting transfers between devices, swap(): return lax.ppermute(value, 'mp', [(0, 1), (1, 0)])  1.05 us
    ppermute x4, waiting for transfers between devices, swap(): return lax.ppermute(value, 'mp', [(0, 1), (1, 0)])  0.87 us
  transfers between devices with their start and end apart: 8, of which 4 were waited for; matrix products, arithmetic and copies ran while one was open for 0% of the time, Pallas kernels for 0%

profile of v4, /device:TPU:7, one launch (start us, length us, event | category | flops | bytes accessed | tf_op | source)
XLA Modules:
  0.0 15.6 jit_solution(7883949704007257518)
XLA Ops:
  0.0 2.3 %project.1 = (f32[64,128]{1,0:T(8,128)S(1)}, s32[1,128]{1,0:T(1,128)S(1)}, bf16[64,512]{1,0:T(8,128)(2,1)S(1)}) custom-call(bf16[128,2048]{1,0:T(8,128)(2,1)} %a_hbm.1, bf16[128,5504]{1,0:T(8,128)(2,1)} %g_hbm.1, bf16[32,2048]{1,0:T(8,128)(2,1)} %bitcast.5, bf16[32,5504]{1,0:T(8,128)(2,1)} %bitcast.4, s32[1,128]{1,0:T(1,128)} %e_hbm.1, s32[1,512]{1,0:T(1,128)} %bitcast.6), custom_call_target="tpu_custom_call" | custom-call | tf_op jit(solution)/shard_map/project/pallas_call | solution.py:78
  2.3 0.7 %collective-permute-start = (f32[64,128]{1,0:T(8,128)S(1)}, f32[64,128]{1,0:T(8,128)S(1)}, u32[]{:S(2)}, u32[]{:S(2)}) collective-permute-start(f32[64,128]{1,0:T(8,128)S(1)} %get-tuple-element.8.mine_ref), channel_id=1, source_target_pairs={{0,1},{1,0},{2,3},{3,2},{4,5},{5,4},{6,7},{7,6},{8,9},{9,8},{10,11... | collective-permute-start | bytes 98312 | tf_op jit(solution)/shard_map/ppermute | solution.py:277
  3.1 0.9 %collective-permute-done.other_ref = f32[64,128]{1,0:T(8,128)S(1)} collective-permute-done((f32[64,128]{1,0:T(8,128)S(1)}, f32[64,128]{1,0:T(8,128)S(1)}, u32[]{:S(2)}, u32[]{:S(2)}) %collective-permute-start) | collective-permute-done | bytes 32800 | tf_op jit(solution)/shard_map/ppermute | solution.py:277
  3.9 0.2 %sketch.1.refs_0_ = bf16[64,128]{1,0:T(8,128)(2,1)S(1)} custom-call(f32[64,128]{1,0:T(8,128)S(1)} %get-tuple-element.8.mine_ref, f32[64,128]{1,0:T(8,128)S(1)} %collective-permute-done.other_ref, s32[1,128]{1,0:T(1,128)S(1)} %get-tuple-element.9.ids_ref), custom_call_target="tpu_custom_call" | custom-call | tf_op jit(solution)/shard_map/sketch/pallas_call | solution.py:125
  4.1 1.6 %collective-permute-start.4 = (bf16[64,128]{1,0:T(8,128)(2,1)S(1)}, bf16[64,128]{1,0:T(8,128)(2,1)S(1)}, u32[]{:S(2)}, u32[]{:S(2)}) collective-permute-start(bf16[64,128]{1,0:T(8,128)(2,1)S(1)} %sketch.1.refs_0_), channel_id=1, source_target_pairs={{0,5},{1,3},{2,9},{3,6},{4,13},{5,10},{6,15},{7,12},{8,11},{9,0},{... | collective-permute-start | bytes 49160 | tf_op jit(solution)/shard_map/ppermute | solution.py:273
  5.7 1.4 %collective-permute-start.3 = (bf16[64,128]{1,0:T(8,128)(2,1)S(1)}, bf16[64,128]{1,0:T(8,128)(2,1)S(1)}, u32[]{:S(2)}, u32[]{:S(2)}) collective-permute-start(bf16[64,128]{1,0:T(8,128)(2,1)S(1)} %sketch.1.refs_0_), channel_id=1, source_target_pairs={{0,9},{1,13},{2,15},{3,10},{4,14},{5,6},{6,2},{7,4},{8,12},{9,5},{... | collective-permute-start | bytes 49160 | tf_op jit(solution)/shard_map/ppermute | solution.py:273
  7.1 2.1 %collective-permute-start.2 = (bf16[64,128]{1,0:T(8,128)(2,1)S(1)}, bf16[64,128]{1,0:T(8,128)(2,1)S(1)}, u32[]{:S(2)}, u32[]{:S(2)}) collective-permute-start(bf16[64,128]{1,0:T(8,128)(2,1)S(1)} %sketch.1.refs_0_), channel_id=1, source_target_pairs={{0,11},{1,15},{2,13},{3,4},{4,9},{5,1},{6,10},{7,0},{8,3},{9,7},{1... | collective-permute-start | bytes 49160 | tf_op jit(solution)/shard_map/ppermute | solution.py:273
  9.3 0.0 collective-permute-start.1
  9.3 0.0 collective-permute-done.4.refs_4_
  9.3 0.2 %collective-permute-start.7 = (bf16[64,128]{1,0:T(8,128)(2,1)S(1)}, bf16[64,128]{1,0:T(8,128)(2,1)S(1)}, u32[]{:S(2)}, u32[]{:S(2)}) collective-permute-start(bf16[64,128]{1,0:T(8,128)(2,1)S(1)} %collective-permute-done.4.refs_4_), channel_id=1, source_target_pairs={{0,1},{1,0},{2,3},{3,2},{4,5},{5,4},{6,7},{7,6},{8,9},{9,8},{10,11... | collective-permute-start | bytes 49160 | tf_op jit(solution)/shard_map/ppermute | solution.py:277
  9.5 2.2 %collective-permute-done.3.refs_3_ = bf16[64,128]{1,0:T(8,128)(2,1)S(1)} collective-permute-done((bf16[64,128]{1,0:T(8,128)(2,1)S(1)}, bf16[64,128]{1,0:T(8,128)(2,1)S(1)}, u32[]{:S(2)}, u32[]{:S(2)}) %collective-permute-start.3) | collective-permute-done | bytes 16416 | tf_op jit(solution)/shard_map/ppermute | solution.py:273
  11.7 0.0 collective-permute-start.6
  11.7 0.4 %collective-permute-done.2.refs_2_ = bf16[64,128]{1,0:T(8,128)(2,1)S(1)} collective-permute-done((bf16[64,128]{1,0:T(8,128)(2,1)S(1)}, bf16[64,128]{1,0:T(8,128)(2,1)S(1)}, u32[]{:S(2)}, u32[]{:S(2)}) %collective-permute-start.2) | collective-permute-done | bytes 16416 | tf_op jit(solution)/shard_map/ppermute | solution.py:273
  12.1 0.1 collective-permute-start.5
  12.2 1.1 %collective-permute-done.1.refs_1_ = bf16[64,128]{1,0:T(8,128)(2,1)S(1)} collective-permute-done((bf16[64,128]{1,0:T(8,128)(2,1)S(1)}, bf16[64,128]{1,0:T(8,128)(2,1)S(1)}, u32[]{:S(2)}, u32[]{:S(2)}) %collective-permute-start.1) | collective-permute-done | bytes 16416 | tf_op jit(solution)/shard_map/ppermute | solution.py:273
  13.3 0.0 collective-permute-done.7.refs_7_
  13.3 0.0 collective-permute-done.6.refs_6_
  13.3 0.0 collective-permute-done.5.refs_5_
  13.3 2.2 %solve.1 = f32[8,512]{1,0:T(8,128)} custom-call(bf16[64,128]{1,0:T(8,128)(2,1)S(1)} %sketch.1.refs_0_, bf16[64,128]{1,0:T(8,128)(2,1)S(1)} %collective-permute-done.1.refs_1_, bf16[64,128]{1,0:T(8,128)(2,1)S(1)} %collective-permute-done.2.refs_2_, bf16[64,128]{1,0:T(8,128)(2,1)S(1)} %collective-permute-done.3.refs_3_, ...), custom_call_target="tpu_custom_call" | custom-call | tf_op jit(solution)/shard_map/solve/pallas_call | solution.py:261
Async XLA Ops:
  2.3 1.6 %collective-permute-start = (f32[64,128]{1,0:T(8,128)S(1)}, f32[64,128]{1,0:T(8,128)S(1)}, u32[]{:S(2)}, u32[]{:S(2)}) collective-permute-start(f32[64,128]{1,0:T(8,128)S(1)} %get-tuple-element.8.mine_ref), channel_id=1, source_target_pairs={{0,1},{1,0},{2,3},{3,2},{4,5},{5,4},{6,7},{7,6},{8,9},{9,8},{10,11... | collective-permute-start | bytes 98312 | tf_op jit(solution)/shard_map/ppermute | solution.py:277
  4.1 5.2 %collective-permute-start.4 = (bf16[64,128]{1,0:T(8,128)(2,1)S(1)}, bf16[64,128]{1,0:T(8,128)(2,1)S(1)}, u32[]{:S(2)}, u32[]{:S(2)}) collective-permute-start(bf16[64,128]{1,0:T(8,128)(2,1)S(1)} %sketch.1.refs_0_), channel_id=1, source_target_pairs={{0,5},{1,3},{2,9},{3,6},{4,13},{5,10},{6,15},{7,12},{8,11},{9,0},{... | collective-permute-start | bytes 49160 | tf_op jit(solution)/shard_map/ppermute | solution.py:273
  5.7 6.0 %collective-permute-start.3 = (bf16[64,128]{1,0:T(8,128)(2,1)S(1)}, bf16[64,128]{1,0:T(8,128)(2,1)S(1)}, u32[]{:S(2)}, u32[]{:S(2)}) collective-permute-start(bf16[64,128]{1,0:T(8,128)(2,1)S(1)} %sketch.1.refs_0_), channel_id=1, source_target_pairs={{0,9},{1,13},{2,15},{3,10},{4,14},{5,6},{6,2},{7,4},{8,12},{9,5},{... | collective-permute-start | bytes 49160 | tf_op jit(solution)/shard_map/ppermute | solution.py:273
  7.1 5.0 %collective-permute-start.2 = (bf16[64,128]{1,0:T(8,128)(2,1)S(1)}, bf16[64,128]{1,0:T(8,128)(2,1)S(1)}, u32[]{:S(2)}, u32[]{:S(2)}) collective-permute-start(bf16[64,128]{1,0:T(8,128)(2,1)S(1)} %sketch.1.refs_0_), channel_id=1, source_target_pairs={{0,11},{1,15},{2,13},{3,4},{4,9},{5,1},{6,10},{7,0},{8,3},{9,7},{1... | collective-permute-start | bytes 49160 | tf_op jit(solution)/shard_map/ppermute | solution.py:273
  9.3 4.1 %collective-permute-start.1 = (bf16[64,128]{1,0:T(8,128)(2,1)S(1)}, bf16[64,128]{1,0:T(8,128)(2,1)S(1)}, u32[]{:S(2)}, u32[]{:S(2)}) collective-permute-start(bf16[64,128]{1,0:T(8,128)(2,1)S(1)} %sketch.1.refs_0_), channel_id=1, source_target_pairs={{0,7},{1,6},{2,1},{3,0},{4,3},{5,2},{6,8},{7,9},{8,15},{9,14},{10,... | collective-permute-start | bytes 49160 | tf_op jit(solution)/shard_map/ppermute | solution.py:273
  9.3 4.1 %collective-permute-start.7 = (bf16[64,128]{1,0:T(8,128)(2,1)S(1)}, bf16[64,128]{1,0:T(8,128)(2,1)S(1)}, u32[]{:S(2)}, u32[]{:S(2)}) collective-permute-start(bf16[64,128]{1,0:T(8,128)(2,1)S(1)} %collective-permute-done.4.refs_4_), channel_id=1, source_target_pairs={{0,1},{1,0},{2,3},{3,2},{4,5},{5,4},{6,7},{7,6},{8,9},{9,8},{10,11... | collective-permute-start | bytes 49160 | tf_op jit(solution)/shard_map/ppermute | solution.py:277
  11.7 1.7 %collective-permute-start.6 = (bf16[64,128]{1,0:T(8,128)(2,1)S(1)}, bf16[64,128]{1,0:T(8,128)(2,1)S(1)}, u32[]{:S(2)}, u32[]{:S(2)}) collective-permute-start(bf16[64,128]{1,0:T(8,128)(2,1)S(1)} %collective-permute-done.3.refs_3_), channel_id=1, source_target_pairs={{0,1},{1,0},{2,3},{3,2},{4,5},{5,4},{6,7},{7,6},{8,9},{9,8},{10,11... | collective-permute-start | bytes 49160 | tf_op jit(solution)/shard_map/ppermute | solution.py:277
  12.1 1.2 %collective-permute-start.5 = (bf16[64,128]{1,0:T(8,128)(2,1)S(1)}, bf16[64,128]{1,0:T(8,128)(2,1)S(1)}, u32[]{:S(2)}, u32[]{:S(2)}) collective-permute-start(bf16[64,128]{1,0:T(8,128)(2,1)S(1)} %collective-permute-done.2.refs_2_), channel_id=1, source_target_pairs={{0,1},{1,0},{2,3},{3,2},{4,5},{5,4},{6,7},{7,6},{8,9},{9,8},{10,11... | collective-permute-start | bytes 49160 | tf_op jit(solution)/shard_map/ppermute | solution.py:277

commit v5 on v4

--- a/solution.py
+++ b/solution.py
@@ -9,10 +9,10 @@
 LANES = 128
 NT = (((1,), (1,)), ((), ()))
 STEPS = (
-    (7, 6, 1, 0, 3, 2, 8, 9, 15, 14, 13, 12, 10, 11, 5, 4),
-    (11, 15, 13, 4, 9, 1, 10, 0, 3, 7, 14, 2, 5, 6, 12, 8),
-    (9, 13, 15, 10, 14, 6, 2, 4, 12, 5, 8, 1, 3, 0, 7, 11),
-    (5, 3, 9, 6, 13, 10, 15, 12, 11, 0, 4, 7, 14, 8, 1, 2),
+    (9, 8, 13, 12, 1, 0, 15, 14, 6, 7, 5, 4, 11, 10, 3, 2),
+    (13, 14, 7, 0, 10, 3, 8, 2, 5, 1, 6, 12, 4, 15, 9, 11),
+    (11, 5, 10, 9, 13, 15, 12, 0, 2, 14, 8, 3, 6, 1, 7, 4),
+    (7, 3, 4, 14, 8, 6, 10, 5, 12, 11, 15, 0, 2, 9, 13, 1),
 )
 
 
@@ -187,7 +187,7 @@
                 inverse = 1.0 / (p * t - q * s)
                 scalings.append((t * inverse, q * inverse, p * inverse, s * inverse))
                 norm = norms[first + which]
-                spread = spread + (down(norm, at) * scalings[-1][0] + down(norm, at + 1) * scalings[-1][2])
+                spread = spread + jnp.abs(down(norm, at) * scalings[-1][0]) + jnp.abs(down(norm, at + 1) * scalings[-1][2])
                 factors = []
                 for k in own:
                     x, y = cols[k][i], cols[k][i + 1]
@@ -233,7 +233,7 @@
 
         out_ref[...] = picked(eye - damping * table[0])
 
-        @pl.when(spread[0, 0] > 4.0 * size)
+        @pl.when(jnp.logical_not(spread[0, 0] <= 4.0 * size))
         def _():
             for k, ref in enumerate(block_refs):
                 basis[k * E_DEV : (k + 1) * E_DEV, 0:k_size] = flat(ref)

time: 15.8 us -> 15.6 us (0.987)
  waiting for transfers between devices: 4.62 us -> 2.56 us
  starting transfers between devices: 6.2 us -> 8.09 us
    ppermute x4, waiting for transfers between devices: 3.75 us -> 1.7 us  [fetch(): return lax.ppermute(value, ('dp', 'mp'), list(enumerate(step)))]
    ppermute x4, starting transfers between devices: 5.15 us -> 6.45 us  [fetch(): return lax.ppermute(value, ('dp', 'mp'), list(enumerate(step)))]
    ppermute x4, starting transfers between devices: 1.05 us -> 1.65 us  [swap(): return lax.ppermute(value, 'mp', [(0, 1), (1, 0)])]
  transfers between devices with their start and end apart: 8 -> 8, of which waited for: 4 -> 3; matrix products, arithmetic and copies ran while one was open for 0% -> 0% of each run, Pallas kernels for 0% -> 0%
where the time goes in v5:
time: 15.6 us; the launch traced here: 15.4 us
  starting transfers between devices  8.09 us (52%)
  Pallas kernels  4.75 us (30%)
  waiting for transfers between devices  2.56 us (16%)
    ppermute x4, starting transfers between devices, fetch(): return lax.ppermute(value, ('dp', 'mp'), list(enumerate(step)))  6.45 us
    pallas_call x1, Pallas kernels, project(): pl.pallas_call(kernel, out_shape=[jax.ShapeDtypeStruct((rin + rout, tok),...  2.34 us
    pallas_call x1, Pallas kernels, solve(): pl.pallas_call(kernel, out_shape=jax.ShapeDtypeStruct((E_DEV, queries), j...  2.25 us
    ppermute x4, waiting for transfers between devices, fetch(): return lax.ppermute(value, ('dp', 'mp'), list(enumerate(step)))  1.7 us
    ppermute x4, starting transfers between devices, swap(): return lax.ppermute(value, 'mp', [(0, 1), (1, 0)])  1.65 us
    ppermute x4, waiting for transfers between devices, swap(): return lax.ppermute(value, 'mp', [(0, 1), (1, 0)])  0.87 us
  transfers between devices with their start and end apart: 8, of which 3 were waited for; matrix products, arithmetic and copies ran while one was open for 0% of the time, Pallas kernels for 0%

profile of v5, /device:TPU:7, one launch (start us, length us, event | category | flops | bytes accessed | tf_op | source)
XLA Modules:
  0.0 15.4 jit_solution(9045077342728397496)
XLA Ops:
  0.0 2.3 %project.1 = (f32[64,128]{1,0:T(8,128)S(1)}, s32[1,128]{1,0:T(1,128)S(1)}, bf16[64,512]{1,0:T(8,128)(2,1)S(1)}) custom-call(bf16[128,2048]{1,0:T(8,128)(2,1)} %a_hbm.1, bf16[128,5504]{1,0:T(8,128)(2,1)} %g_hbm.1, bf16[32,2048]{1,0:T(8,128)(2,1)} %bitcast.5, bf16[32,5504]{1,0:T(8,128)(2,1)} %bitcast.4, s32[1,128]{1,0:T(1,128)} %e_hbm.1, s32[1,512]{1,0:T(1,128)} %bitcast.6), custom_call_target="tpu_custom_call" | custom-call | tf_op jit(solution)/shard_map/project/pallas_call | solution.py:78
  2.3 0.7 %collective-permute-start = (f32[64,128]{1,0:T(8,128)S(1)}, f32[64,128]{1,0:T(8,128)S(1)}, u32[]{:S(2)}, u32[]{:S(2)}) collective-permute-start(f32[64,128]{1,0:T(8,128)S(1)} %get-tuple-element.8.mine_ref), channel_id=1, source_target_pairs={{0,1},{1,0},{2,3},{3,2},{4,5},{5,4},{6,7},{7,6},{8,9},{9,8},{10,11... | collective-permute-start | bytes 98312 | tf_op jit(solution)/shard_map/ppermute | solution.py:277
  3.1 0.9 %collective-permute-done.other_ref = f32[64,128]{1,0:T(8,128)S(1)} collective-permute-done((f32[64,128]{1,0:T(8,128)S(1)}, f32[64,128]{1,0:T(8,128)S(1)}, u32[]{:S(2)}, u32[]{:S(2)}) %collective-permute-start) | collective-permute-done | bytes 32800 | tf_op jit(solution)/shard_map/ppermute | solution.py:277
  3.9 0.2 %sketch.1.refs_0_ = bf16[64,128]{1,0:T(8,128)(2,1)S(1)} custom-call(f32[64,128]{1,0:T(8,128)S(1)} %get-tuple-element.8.mine_ref, f32[64,128]{1,0:T(8,128)S(1)} %collective-permute-done.other_ref, s32[1,128]{1,0:T(1,128)S(1)} %get-tuple-element.9.ids_ref), custom_call_target="tpu_custom_call" | custom-call | tf_op jit(solution)/shard_map/sketch/pallas_call | solution.py:125
  4.1 3.6 %collective-permute-start.4 = (bf16[64,128]{1,0:T(8,128)(2,1)S(1)}, bf16[64,128]{1,0:T(8,128)(2,1)S(1)}, u32[]{:S(2)}, u32[]{:S(2)}) collective-permute-start(bf16[64,128]{1,0:T(8,128)(2,1)S(1)} %sketch.1.refs_0_), channel_id=1, source_target_pairs={{0,7},{1,3},{2,4},{3,14},{4,8},{5,6},{6,10},{7,5},{8,12},{9,11},{1... | collective-permute-start | bytes 49160 | tf_op jit(solution)/shard_map/ppermute | solution.py:273
  7.7 0.0 collective-permute-start.3
  7.7 0.5 %collective-permute-start.2 = (bf16[64,128]{1,0:T(8,128)(2,1)S(1)}, bf16[64,128]{1,0:T(8,128)(2,1)S(1)}, u32[]{:S(2)}, u32[]{:S(2)}) collective-permute-start(bf16[64,128]{1,0:T(8,128)(2,1)S(1)} %sketch.1.refs_0_), channel_id=1, source_target_pairs={{0,13},{1,14},{2,7},{3,0},{4,10},{5,3},{6,8},{7,2},{8,5},{9,1},{10... | collective-permute-start | bytes 49160 | tf_op jit(solution)/shard_map/ppermute | solution.py:273
  8.2 2.4 %collective-permute-start.1 = (bf16[64,128]{1,0:T(8,128)(2,1)S(1)}, bf16[64,128]{1,0:T(8,128)(2,1)S(1)}, u32[]{:S(2)}, u32[]{:S(2)}) collective-permute-start(bf16[64,128]{1,0:T(8,128)(2,1)S(1)} %sketch.1.refs_0_), channel_id=1, source_target_pairs={{0,9},{1,8},{2,13},{3,12},{4,1},{5,0},{6,15},{7,14},{8,6},{9,7},{1... | collective-permute-start | bytes 49160 | tf_op jit(solution)/shard_map/ppermute | solution.py:273
  10.6 0.0 collective-permute-done.4.refs_4_
  10.6 0.4 %collective-permute-start.7 = (bf16[64,128]{1,0:T(8,128)(2,1)S(1)}, bf16[64,128]{1,0:T(8,128)(2,1)S(1)}, u32[]{:S(2)}, u32[]{:S(2)}) collective-permute-start(bf16[64,128]{1,0:T(8,128)(2,1)S(1)} %collective-permute-done.4.refs_4_), channel_id=1, source_target_pairs={{0,1},{1,0},{2,3},{3,2},{4,5},{5,4},{6,7},{7,6},{8,9},{9,8},{10,11... | collective-permute-start | bytes 49160 | tf_op jit(solution)/shard_map/ppermute | solution.py:277
  11.0 0.3 %collective-permute-done.3.refs_3_ = bf16[64,128]{1,0:T(8,128)(2,1)S(1)} collective-permute-done((bf16[64,128]{1,0:T(8,128)(2,1)S(1)}, bf16[64,128]{1,0:T(8,128)(2,1)S(1)}, u32[]{:S(2)}, u32[]{:S(2)}) %collective-permute-start.3) | collective-permute-done | bytes 16416 | tf_op jit(solution)/shard_map/ppermute | solution.py:273
  11.2 0.4 %collective-permute-start.6 = (bf16[64,128]{1,0:T(8,128)(2,1)S(1)}, bf16[64,128]{1,0:T(8,128)(2,1)S(1)}, u32[]{:S(2)}, u32[]{:S(2)}) collective-permute-start(bf16[64,128]{1,0:T(8,128)(2,1)S(1)} %collective-permute-done.3.refs_3_), channel_id=1, source_target_pairs={{0,1},{1,0},{2,3},{3,2},{4,5},{5,4},{6,7},{7,6},{8,9},{9,8},{10,11... | collective-permute-start | bytes 49160 | tf_op jit(solution)/shard_map/ppermute | solution.py:277
  11.6 0.0 collective-permute-done.2.refs_2_
  11.6 0.1 collective-permute-start.5
  11.7 1.4 %collective-permute-done.1.refs_1_ = bf16[64,128]{1,0:T(8,128)(2,1)S(1)} collective-permute-done((bf16[64,128]{1,0:T(8,128)(2,1)S(1)}, bf16[64,128]{1,0:T(8,128)(2,1)S(1)}, u32[]{:S(2)}, u32[]{:S(2)}) %collective-permute-start.1) | collective-permute-done | bytes 16416 | tf_op jit(solution)/shard_map/ppermute | solution.py:273
  13.2 0.0 collective-permute-done.7.refs_7_
  13.2 0.0 collective-permute-done.6.refs_6_
  13.2 0.0 collective-permute-done.5.refs_5_
  13.2 2.3 %solve.1 = f32[8,512]{1,0:T(8,128)} custom-call(bf16[64,128]{1,0:T(8,128)(2,1)S(1)} %sketch.1.refs_0_, bf16[64,128]{1,0:T(8,128)(2,1)S(1)} %collective-permute-done.1.refs_1_, bf16[64,128]{1,0:T(8,128)(2,1)S(1)} %collective-permute-done.2.refs_2_, bf16[64,128]{1,0:T(8,128)(2,1)S(1)} %collective-permute-done.3.refs_3_, ...), custom_call_target="tpu_custom_call" | custom-call | tf_op jit(solution)/shard_map/solve/pallas_call | solution.py:261
Async XLA Ops:
  2.3 1.6 %collective-permute-start = (f32[64,128]{1,0:T(8,128)S(1)}, f32[64,128]{1,0:T(8,128)S(1)}, u32[]{:S(2)}, u32[]{:S(2)}) collective-permute-start(f32[64,128]{1,0:T(8,128)S(1)} %get-tuple-element.8.mine_ref), channel_id=1, source_target_pairs={{0,1},{1,0},{2,3},{3,2},{4,5},{5,4},{6,7},{7,6},{8,9},{9,8},{10,11... | collective-permute-start | bytes 98312 | tf_op jit(solution)/shard_map/ppermute | solution.py:277
  4.1 6.5 %collective-permute-start.4 = (bf16[64,128]{1,0:T(8,128)(2,1)S(1)}, bf16[64,128]{1,0:T(8,128)(2,1)S(1)}, u32[]{:S(2)}, u32[]{:S(2)}) collective-permute-start(bf16[64,128]{1,0:T(8,128)(2,1)S(1)} %sketch.1.refs_0_), channel_id=1, source_target_pairs={{0,7},{1,3},{2,4},{3,14},{4,8},{5,6},{6,10},{7,5},{8,12},{9,11},{1... | collective-permute-start | bytes 49160 | tf_op jit(solution)/shard_map/ppermute | solution.py:273
  7.7 3.5 %collective-permute-start.3 = (bf16[64,128]{1,0:T(8,128)(2,1)S(1)}, bf16[64,128]{1,0:T(8,128)(2,1)S(1)}, u32[]{:S(2)}, u32[]{:S(2)}) collective-permute-start(bf16[64,128]{1,0:T(8,128)(2,1)S(1)} %sketch.1.refs_0_), channel_id=1, source_target_pairs={{0,11},{1,5},{2,10},{3,9},{4,13},{5,15},{6,12},{7,0},{8,2},{9,14},... | collective-permute-start | bytes 49160 | tf_op jit(solution)/shard_map/ppermute | solution.py:273
  7.7 3.9 %collective-permute-start.2 = (bf16[64,128]{1,0:T(8,128)(2,1)S(1)}, bf16[64,128]{1,0:T(8,128)(2,1)S(1)}, u32[]{:S(2)}, u32[]{:S(2)}) collective-permute-start(bf16[64,128]{1,0:T(8,128)(2,1)S(1)} %sketch.1.refs_0_), channel_id=1, source_target_pairs={{0,13},{1,14},{2,7},{3,0},{4,10},{5,3},{6,8},{7,2},{8,5},{9,1},{10... | collective-permute-start | bytes 49160 | tf_op jit(solution)/shard_map/ppermute | solution.py:273
  8.2 5.0 %collective-permute-start.1 = (bf16[64,128]{1,0:T(8,128)(2,1)S(1)}, bf16[64,128]{1,0:T(8,128)(2,1)S(1)}, u32[]{:S(2)}, u32[]{:S(2)}) collective-permute-start(bf16[64,128]{1,0:T(8,128)(2,1)S(1)} %sketch.1.refs_0_), channel_id=1, source_target_pairs={{0,9},{1,8},{2,13},{3,12},{4,1},{5,0},{6,15},{7,14},{8,6},{9,7},{1... | collective-permute-start | bytes 49160 | tf_op jit(solution)/shard_map/ppermute | solution.py:273
  10.6 2.6 %collective-permute-start.7 = (bf16[64,128]{1,0:T(8,128)(2,1)S(1)}, bf16[64,128]{1,0:T(8,128)(2,1)S(1)}, u32[]{:S(2)}, u32[]{:S(2)}) collective-permute-start(bf16[64,128]{1,0:T(8,128)(2,1)S(1)} %collective-permute-done.4.refs_4_), channel_id=1, source_target_pairs={{0,1},{1,0},{2,3},{3,2},{4,5},{5,4},{6,7},{7,6},{8,9},{9,8},{10,11... | collective-permute-start | bytes 49160 | tf_op jit(solution)/shard_map/ppermute | solution.py:277
  11.2 2.0 %collective-permute-start.6 = (bf16[64,128]{1,0:T(8,128)(2,1)S(1)}, bf16[64,128]{1,0:T(8,128)(2,1)S(1)}, u32[]{:S(2)}, u32[]{:S(2)}) collective-permute-start(bf16[64,128]{1,0:T(8,128)(2,1)S(1)} %collective-permute-done.3.refs_3_), channel_id=1, source_target_pairs={{0,1},{1,0},{2,3},{3,2},{4,5},{5,4},{6,7},{7,6},{8,9},{9,8},{10,11... | collective-permute-start | bytes 49160 | tf_op jit(solution)/shard_map/ppermute | solution.py:277
  11.6 1.6 %collective-permute-start.5 = (bf16[64,128]{1,0:T(8,128)(2,1)S(1)}, bf16[64,128]{1,0:T(8,128)(2,1)S(1)}, u32[]{:S(2)}, u32[]{:S(2)}) collective-permute-start(bf16[64,128]{1,0:T(8,128)(2,1)S(1)} %collective-permute-done.2.refs_2_), channel_id=1, source_target_pairs={{0,1},{1,0},{2,3},{3,2},{4,5},{5,4},{6,7},{7,6},{8,9},{9,8},{10,11... | collective-permute-start | bytes 49160 | tf_op jit(solution)/shard_map/ppermute | solution.py:277

commit v6 on v5

--- a/solution.py
+++ b/solution.py
@@ -170,10 +170,14 @@
         def down(value, i):
             return jnp.broadcast_to(value[i : i + 1], shape)
 
-        for first in range(0, count, group):
+        left = set(range(count))
+        for first in [*range(group, count, group), 0]:
             own = range(group)
             base = size + first * E_DEV
-            wide = [[jnp.broadcast_to(t[:, c : c + 1], shape) for c in range(base, base + span)] for t in table]
+            wide = {
+                r: [jnp.broadcast_to(table[r][:, c : c + 1], shape) for c in range(base, base + span)] for r in sorted(left)
+            }
+            left -= {first + k for k in own}
             rows = [table[first + k] + jnp.where(lane == sub + (base + k * E_DEV), damping, 0.0) for k in own]
             cols = [list(wide[first + k]) for k in own]
             for j in range(span):
@@ -214,12 +218,11 @@
                     scaled = jnp.where(here[at + 1], c * lower - d * upper, scaled)
                 table[first + k] = scaled
             lines = [down(table[first + j // E_DEV], j % E_DEV) for j in range(span)]
-            for r in range(count):
-                if not first <= r < first + group:
-                    terms = [wide[r][j] * lines[j] for j in range(span)]
-                    while len(terms) > 1:
-                        terms = [x + y for x, y in zip(terms[::2], terms[1::2])]
-                    table[r] = table[r] - terms[0]
+            for r in sorted(left):
+                terms = [wide[r][j] * lines[j] for j in range(span)]
+                while len(terms) > 1:
+                    terms = [x + y for x, y in zip(terms[::2], terms[1::2])]
+                table[r] = table[r] - terms[0]
 
         eye = jnp.where(sub == lane, 1.0, 0.0)
 

time: 15.6 us -> 15.6 us (level)
  no operation moved by 1% of the time
where the time goes in v6:
time: 15.6 us; the launch traced here: 15.4 us
  starting transfers between devices  8.09 us (52%)
  Pallas kernels  4.72 us (30%)
  waiting for transfers between devices  2.56 us (16%)
    ppermute x4, starting transfers between devices, fetch(): return lax.ppermute(value, ('dp', 'mp'), list(enumerate(step)))  6.45 us
    pallas_call x1, Pallas kernels, project(): pl.pallas_call(kernel, out_shape=[jax.ShapeDtypeStruct((rin + rout, tok),...  2.34 us
    pallas_call x1, Pallas kernels, solve(): pl.pallas_call(kernel, out_shape=jax.ShapeDtypeStruct((E_DEV, queries), j...  2.23 us
    ppermute x4, waiting for transfers between devices, fetch(): return lax.ppermute(value, ('dp', 'mp'), list(enumerate(step)))  1.7 us
    ppermute x4, starting transfers between devices, swap(): return lax.ppermute(value, 'mp', [(0, 1), (1, 0)])  1.65 us
    ppermute x4, waiting for transfers between devices, swap(): return lax.ppermute(value, 'mp', [(0, 1), (1, 0)])  0.87 us
  transfers between devices with their start and end apart: 8, of which 3 were waited for; matrix products, arithmetic and copies ran while one was open for 0% of the time, Pallas kernels for 0%

profile of v6, /device:TPU:7, one launch (start us, length us, event | category | flops | bytes accessed | tf_op | source)
XLA Modules:
  0.0 15.4 jit_solution(6782485745069970491)
XLA Ops:
  0.0 2.3 %project.1 = (f32[64,128]{1,0:T(8,128)S(1)}, s32[1,128]{1,0:T(1,128)S(1)}, bf16[64,512]{1,0:T(8,128)(2,1)S(1)}) custom-call(bf16[128,2048]{1,0:T(8,128)(2,1)} %a_hbm.1, bf16[128,5504]{1,0:T(8,128)(2,1)} %g_hbm.1, bf16[32,2048]{1,0:T(8,128)(2,1)} %bitcast.5, bf16[32,5504]{1,0:T(8,128)(2,1)} %bitcast.4, s32[1,128]{1,0:T(1,128)} %e_hbm.1, s32[1,512]{1,0:T(1,128)} %bitcast.6), custom_call_target="tpu_custom_call" | custom-call | tf_op jit(solution)/shard_map/project/pallas_call | solution.py:78
  2.3 0.7 %collective-permute-start = (f32[64,128]{1,0:T(8,128)S(1)}, f32[64,128]{1,0:T(8,128)S(1)}, u32[]{:S(2)}, u32[]{:S(2)}) collective-permute-start(f32[64,128]{1,0:T(8,128)S(1)} %get-tuple-element.8.mine_ref), channel_id=1, source_target_pairs={{0,1},{1,0},{2,3},{3,2},{4,5},{5,4},{6,7},{7,6},{8,9},{9,8},{10,11... | collective-permute-start | bytes 98312 | tf_op jit(solution)/shard_map/ppermute | solution.py:280
  3.1 0.9 %collective-permute-done.other_ref = f32[64,128]{1,0:T(8,128)S(1)} collective-permute-done((f32[64,128]{1,0:T(8,128)S(1)}, f32[64,128]{1,0:T(8,128)S(1)}, u32[]{:S(2)}, u32[]{:S(2)}) %collective-permute-start) | collective-permute-done | bytes 32800 | tf_op jit(solution)/shard_map/ppermute | solution.py:280
  3.9 0.2 %sketch.1.refs_0_ = bf16[64,128]{1,0:T(8,128)(2,1)S(1)} custom-call(f32[64,128]{1,0:T(8,128)S(1)} %get-tuple-element.8.mine_ref, f32[64,128]{1,0:T(8,128)S(1)} %collective-permute-done.other_ref, s32[1,128]{1,0:T(1,128)S(1)} %get-tuple-element.9.ids_ref), custom_call_target="tpu_custom_call" | custom-call | tf_op jit(solution)/shard_map/sketch/pallas_call | solution.py:125
  4.1 3.6 %collective-permute-start.4 = (bf16[64,128]{1,0:T(8,128)(2,1)S(1)}, bf16[64,128]{1,0:T(8,128)(2,1)S(1)}, u32[]{:S(2)}, u32[]{:S(2)}) collective-permute-start(bf16[64,128]{1,0:T(8,128)(2,1)S(1)} %sketch.1.refs_0_), channel_id=1, source_target_pairs={{0,7},{1,3},{2,4},{3,14},{4,8},{5,6},{6,10},{7,5},{8,12},{9,11},{1... | collective-permute-start | bytes 49160 | tf_op jit(solution)/shard_map/ppermute | solution.py:276
  7.7 0.0 collective-permute-start.3
  7.7 0.5 %collective-permute-start.2 = (bf16[64,128]{1,0:T(8,128)(2,1)S(1)}, bf16[64,128]{1,0:T(8,128)(2,1)S(1)}, u32[]{:S(2)}, u32[]{:S(2)}) collective-permute-start(bf16[64,128]{1,0:T(8,128)(2,1)S(1)} %sketch.1.refs_0_), channel_id=1, source_target_pairs={{0,13},{1,14},{2,7},{3,0},{4,10},{5,3},{6,8},{7,2},{8,5},{9,1},{10... | collective-permute-start | bytes 49160 | tf_op jit(solution)/shard_map/ppermute | solution.py:276
  8.2 2.4 %collective-permute-start.1 = (bf16[64,128]{1,0:T(8,128)(2,1)S(1)}, bf16[64,128]{1,0:T(8,128)(2,1)S(1)}, u32[]{:S(2)}, u32[]{:S(2)}) collective-permute-start(bf16[64,128]{1,0:T(8,128)(2,1)S(1)} %sketch.1.refs_0_), channel_id=1, source_target_pairs={{0,9},{1,8},{2,13},{3,12},{4,1},{5,0},{6,15},{7,14},{8,6},{9,7},{1... | collective-permute-start | bytes 49160 | tf_op jit(solution)/shard_map/ppermute | solution.py:276
  10.6 0.0 collective-permute-done.4.refs_4_
  10.6 0.4 %collective-permute-start.7 = (bf16[64,128]{1,0:T(8,128)(2,1)S(1)}, bf16[64,128]{1,0:T(8,128)(2,1)S(1)}, u32[]{:S(2)}, u32[]{:S(2)}) collective-permute-start(bf16[64,128]{1,0:T(8,128)(2,1)S(1)} %collective-permute-done.4.refs_4_), channel_id=1, source_target_pairs={{0,1},{1,0},{2,3},{3,2},{4,5},{5,4},{6,7},{7,6},{8,9},{9,8},{10,11... | collective-permute-start | bytes 49160 | tf_op jit(solution)/shard_map/ppermute | solution.py:280
  11.0 0.3 %collective-permute-done.3.refs_3_ = bf16[64,128]{1,0:T(8,128)(2,1)S(1)} collective-permute-done((bf16[64,128]{1,0:T(8,128)(2,1)S(1)}, bf16[64,128]{1,0:T(8,128)(2,1)S(1)}, u32[]{:S(2)}, u32[]{:S(2)}) %collective-permute-start.3) | collective-permute-done | bytes 16416 | tf_op jit(solution)/shard_map/ppermute | solution.py:276
  11.2 0.4 %collective-permute-start.6 = (bf16[64,128]{1,0:T(8,128)(2,1)S(1)}, bf16[64,128]{1,0:T(8,128)(2,1)S(1)}, u32[]{:S(2)}, u32[]{:S(2)}) collective-permute-start(bf16[64,128]{1,0:T(8,128)(2,1)S(1)} %collective-permute-done.3.refs_3_), channel_id=1, source_target_pairs={{0,1},{1,0},{2,3},{3,2},{4,5},{5,4},{6,7},{7,6},{8,9},{9,8},{10,11... | collective-permute-start | bytes 49160 | tf_op jit(solution)/shard_map/ppermute | solution.py:280
  11.6 0.0 collective-permute-done.2.refs_2_
  11.6 0.1 collective-permute-start.5
  11.7 1.4 %collective-permute-done.1.refs_1_ = bf16[64,128]{1,0:T(8,128)(2,1)S(1)} collective-permute-done((bf16[64,128]{1,0:T(8,128)(2,1)S(1)}, bf16[64,128]{1,0:T(8,128)(2,1)S(1)}, u32[]{:S(2)}, u32[]{:S(2)}) %collective-permute-start.1) | collective-permute-done | bytes 16416 | tf_op jit(solution)/shard_map/ppermute | solution.py:276
  13.2 0.0 collective-permute-done.7.refs_7_
  13.2 0.0 collective-permute-done.6.refs_6_
  13.2 0.0 collective-permute-done.5.refs_5_
  13.2 2.2 %solve.1 = f32[8,512]{1,0:T(8,128)} custom-call(bf16[64,128]{1,0:T(8,128)(2,1)S(1)} %sketch.1.refs_0_, bf16[64,128]{1,0:T(8,128)(2,1)S(1)} %collective-permute-done.1.refs_1_, bf16[64,128]{1,0:T(8,128)(2,1)S(1)} %collective-permute-done.2.refs_2_, bf16[64,128]{1,0:T(8,128)(2,1)S(1)} %collective-permute-done.3.refs_3_, ...), custom_call_target="tpu_custom_call" | custom-call | tf_op jit(solution)/shard_map/solve/pallas_call | solution.py:264
Async XLA Ops:
  2.3 1.6 %collective-permute-start = (f32[64,128]{1,0:T(8,128)S(1)}, f32[64,128]{1,0:T(8,128)S(1)}, u32[]{:S(2)}, u32[]{:S(2)}) collective-permute-start(f32[64,128]{1,0:T(8,128)S(1)} %get-tuple-element.8.mine_ref), channel_id=1, source_target_pairs={{0,1},{1,0},{2,3},{3,2},{4,5},{5,4},{6,7},{7,6},{8,9},{9,8},{10,11... | collective-permute-start | bytes 98312 | tf_op jit(solution)/shard_map/ppermute | solution.py:280
  4.1 6.5 %collective-permute-start.4 = (bf16[64,128]{1,0:T(8,128)(2,1)S(1)}, bf16[64,128]{1,0:T(8,128)(2,1)S(1)}, u32[]{:S(2)}, u32[]{:S(2)}) collective-permute-start(bf16[64,128]{1,0:T(8,128)(2,1)S(1)} %sketch.1.refs_0_), channel_id=1, source_target_pairs={{0,7},{1,3},{2,4},{3,14},{4,8},{5,6},{6,10},{7,5},{8,12},{9,11},{1... | collective-permute-start | bytes 49160 | tf_op jit(solution)/shard_map/ppermute | solution.py:276
  7.7 3.5 %collective-permute-start.3 = (bf16[64,128]{1,0:T(8,128)(2,1)S(1)}, bf16[64,128]{1,0:T(8,128)(2,1)S(1)}, u32[]{:S(2)}, u32[]{:S(2)}) collective-permute-start(bf16[64,128]{1,0:T(8,128)(2,1)S(1)} %sketch.1.refs_0_), channel_id=1, source_target_pairs={{0,11},{1,5},{2,10},{3,9},{4,13},{5,15},{6,12},{7,0},{8,2},{9,14},... | collective-permute-start | bytes 49160 | tf_op jit(solution)/shard_map/ppermute | solution.py:276
  7.7 3.9 %collective-permute-start.2 = (bf16[64,128]{1,0:T(8,128)(2,1)S(1)}, bf16[64,128]{1,0:T(8,128)(2,1)S(1)}, u32[]{:S(2)}, u32[]{:S(2)}) collective-permute-start(bf16[64,128]{1,0:T(8,128)(2,1)S(1)} %sketch.1.refs_0_), channel_id=1, source_target_pairs={{0,13},{1,14},{2,7},{3,0},{4,10},{5,3},{6,8},{7,2},{8,5},{9,1},{10... | collective-permute-start | bytes 49160 | tf_op jit(solution)/shard_map/ppermute | solution.py:276
  8.2 5.0 %collective-permute-start.1 = (bf16[64,128]{1,0:T(8,128)(2,1)S(1)}, bf16[64,128]{1,0:T(8,128)(2,1)S(1)}, u32[]{:S(2)}, u32[]{:S(2)}) collective-permute-start(bf16[64,128]{1,0:T(8,128)(2,1)S(1)} %sketch.1.refs_0_), channel_id=1, source_target_pairs={{0,9},{1,8},{2,13},{3,12},{4,1},{5,0},{6,15},{7,14},{8,6},{9,7},{1... | collective-permute-start | bytes 49160 | tf_op jit(solution)/shard_map/ppermute | solution.py:276
  10.6 2.6 %collective-permute-start.7 = (bf16[64,128]{1,0:T(8,128)(2,1)S(1)}, bf16[64,128]{1,0:T(8,128)(2,1)S(1)}, u32[]{:S(2)}, u32[]{:S(2)}) collective-permute-start(bf16[64,128]{1,0:T(8,128)(2,1)S(1)} %collective-permute-done.4.refs_4_), channel_id=1, source_target_pairs={{0,1},{1,0},{2,3},{3,2},{4,5},{5,4},{6,7},{7,6},{8,9},{9,8},{10,11... | collective-permute-start | bytes 49160 | tf_op jit(solution)/shard_map/ppermute | solution.py:280
  11.2 2.0 %collective-permute-start.6 = (bf16[64,128]{1,0:T(8,128)(2,1)S(1)}, bf16[64,128]{1,0:T(8,128)(2,1)S(1)}, u32[]{:S(2)}, u32[]{:S(2)}) collective-permute-start(bf16[64,128]{1,0:T(8,128)(2,1)S(1)} %collective-permute-done.3.refs_3_), channel_id=1, source_target_pairs={{0,1},{1,0},{2,3},{3,2},{4,5},{5,4},{6,7},{7,6},{8,9},{9,8},{10,11... | collective-permute-start | bytes 49160 | tf_op jit(solution)/shard_map/ppermute | solution.py:280
  11.6 1.6 %collective-permute-start.5 = (bf16[64,128]{1,0:T(8,128)(2,1)S(1)}, bf16[64,128]{1,0:T(8,128)(2,1)S(1)}, u32[]{:S(2)}, u32[]{:S(2)}) collective-permute-start(bf16[64,128]{1,0:T(8,128)(2,1)S(1)} %collective-permute-done.2.refs_2_), channel_id=1, source_target_pairs={{0,1},{1,0},{2,3},{3,2},{4,5},{5,4},{6,7},{7,6},{8,9},{9,8},{10,11... | collective-permute-start | bytes 49160 | tf_op jit(solution)/shard_map/ppermute | solution.py:280

commit v7 on v6

--- a/solution.py
+++ b/solution.py
@@ -187,7 +187,7 @@
             for i in range(0, span, 2):
                 which, at = i // E_DEV, i % E_DEV
                 p, q = down(cols[which][i], at), down(cols[which][i + 1], at)
-                s, t = down(cols[which][i], at + 1), down(cols[which][i + 1], at + 1)
+                s, t = q, down(cols[which][i + 1], at + 1)
                 inverse = 1.0 / (p * t - q * s)
                 scalings.append((t * inverse, q * inverse, p * inverse, s * inverse))
                 norm = norms[first + which]

time: 15.6 us -> 15.6 us (level)
  no operation moved by 1% of the time
where the time goes in v7:
time: 15.6 us; the launch traced here: 15.4 us
  starting transfers between devices  8.09 us (52%)
  Pallas kernels  4.71 us (30%)
  waiting for transfers between devices  2.56 us (16%)
    ppermute x4, starting transfers between devices, fetch(): return lax.ppermute(value, ('dp', 'mp'), list(enumerate(step)))  6.45 us
    pallas_call x1, Pallas kernels, project(): pl.pallas_call(kernel, out_shape=[jax.ShapeDtypeStruct((rin + rout, tok),...  2.34 us
    pallas_call x1, Pallas kernels, solve(): pl.pallas_call(kernel, out_shape=jax.ShapeDtypeStruct((E_DEV, queries), j...  2.22 us
    ppermute x4, waiting for transfers between devices, fetch(): return lax.ppermute(value, ('dp', 'mp'), list(enumerate(step)))  1.7 us
    ppermute x4, starting transfers between devices, swap(): return lax.ppermute(value, 'mp', [(0, 1), (1, 0)])  1.65 us
    ppermute x4, waiting for transfers between devices, swap(): return lax.ppermute(value, 'mp', [(0, 1), (1, 0)])  0.87 us
  transfers between devices with their start and end apart: 8, of which 3 were waited for; matrix products, arithmetic and copies ran while one was open for 0% of the time, Pallas kernels for 0%

profile of v7, /device:TPU:7, one launch (start us, length us, event | category | flops | bytes accessed | tf_op | source)
XLA Modules:
  0.0 15.4 jit_solution(8322407311870373428)
XLA Ops:
  0.0 2.3 %project.1 = (f32[64,128]{1,0:T(8,128)S(1)}, s32[1,128]{1,0:T(1,128)S(1)}, bf16[64,512]{1,0:T(8,128)(2,1)S(1)}) custom-call(bf16[128,2048]{1,0:T(8,128)(2,1)} %a_hbm.1, bf16[128,5504]{1,0:T(8,128)(2,1)} %g_hbm.1, bf16[32,2048]{1,0:T(8,128)(2,1)} %bitcast.5, bf16[32,5504]{1,0:T(8,128)(2,1)} %bitcast.4, s32[1,128]{1,0:T(1,128)} %e_hbm.1, s32[1,512]{1,0:T(1,128)} %bitcast.6), custom_call_target="tpu_custom_call" | custom-call | tf_op jit(solution)/shard_map/project/pallas_call | solution.py:78
  2.3 0.7 %collective-permute-start = (f32[64,128]{1,0:T(8,128)S(1)}, f32[64,128]{1,0:T(8,128)S(1)}, u32[]{:S(2)}, u32[]{:S(2)}) collective-permute-start(f32[64,128]{1,0:T(8,128)S(1)} %get-tuple-element.8.mine_ref), channel_id=1, source_target_pairs={{0,1},{1,0},{2,3},{3,2},{4,5},{5,4},{6,7},{7,6},{8,9},{9,8},{10,11... | collective-permute-start | bytes 98312 | tf_op jit(solution)/shard_map/ppermute | solution.py:280
  3.1 0.9 %collective-permute-done.other_ref = f32[64,128]{1,0:T(8,128)S(1)} collective-permute-done((f32[64,128]{1,0:T(8,128)S(1)}, f32[64,128]{1,0:T(8,128)S(1)}, u32[]{:S(2)}, u32[]{:S(2)}) %collective-permute-start) | collective-permute-done | bytes 32800 | tf_op jit(solution)/shard_map/ppermute | solution.py:280
  3.9 0.2 %sketch.1.refs_0_ = bf16[64,128]{1,0:T(8,128)(2,1)S(1)} custom-call(f32[64,128]{1,0:T(8,128)S(1)} %get-tuple-element.8.mine_ref, f32[64,128]{1,0:T(8,128)S(1)} %collective-permute-done.other_ref, s32[1,128]{1,0:T(1,128)S(1)} %get-tuple-element.9.ids_ref), custom_call_target="tpu_custom_call" | custom-call | tf_op jit(solution)/shard_map/sketch/pallas_call | solution.py:125
  4.1 3.6 %collective-permute-start.4 = (bf16[64,128]{1,0:T(8,128)(2,1)S(1)}, bf16[64,128]{1,0:T(8,128)(2,1)S(1)}, u32[]{:S(2)}, u32[]{:S(2)}) collective-permute-start(bf16[64,128]{1,0:T(8,128)(2,1)S(1)} %sketch.1.refs_0_), channel_id=1, source_target_pairs={{0,7},{1,3},{2,4},{3,14},{4,8},{5,6},{6,10},{7,5},{8,12},{9,11},{1... | collective-permute-start | bytes 49160 | tf_op jit(solution)/shard_map/ppermute | solution.py:276
  7.7 0.0 collective-permute-start.3
  7.7 0.5 %collective-permute-start.2 = (bf16[64,128]{1,0:T(8,128)(2,1)S(1)}, bf16[64,128]{1,0:T(8,128)(2,1)S(1)}, u32[]{:S(2)}, u32[]{:S(2)}) collective-permute-start(bf16[64,128]{1,0:T(8,128)(2,1)S(1)} %sketch.1.refs_0_), channel_id=1, source_target_pairs={{0,13},{1,14},{2,7},{3,0},{4,10},{5,3},{6,8},{7,2},{8,5},{9,1},{10... | collective-permute-start | bytes 49160 | tf_op jit(solution)/shard_map/ppermute | solution.py:276
  8.2 2.4 %collective-permute-start.1 = (bf16[64,128]{1,0:T(8,128)(2,1)S(1)}, bf16[64,128]{1,0:T(8,128)(2,1)S(1)}, u32[]{:S(2)}, u32[]{:S(2)}) collective-permute-start(bf16[64,128]{1,0:T(8,128)(2,1)S(1)} %sketch.1.refs_0_), channel_id=1, source_target_pairs={{0,9},{1,8},{2,13},{3,12},{4,1},{5,0},{6,15},{7,14},{8,6},{9,7},{1... | collective-permute-start | bytes 49160 | tf_op jit(solution)/shard_map/ppermute | solution.py:276
  10.6 0.0 collective-permute-done.4.refs_4_
  10.6 0.4 %collective-permute-start.7 = (bf16[64,128]{1,0:T(8,128)(2,1)S(1)}, bf16[64,128]{1,0:T(8,128)(2,1)S(1)}, u32[]{:S(2)}, u32[]{:S(2)}) collective-permute-start(bf16[64,128]{1,0:T(8,128)(2,1)S(1)} %collective-permute-done.4.refs_4_), channel_id=1, source_target_pairs={{0,1},{1,0},{2,3},{3,2},{4,5},{5,4},{6,7},{7,6},{8,9},{9,8},{10,11... | collective-permute-start | bytes 49160 | tf_op jit(solution)/shard_map/ppermute | solution.py:280
  11.0 0.3 %collective-permute-done.3.refs_3_ = bf16[64,128]{1,0:T(8,128)(2,1)S(1)} collective-permute-done((bf16[64,128]{1,0:T(8,128)(2,1)S(1)}, bf16[64,128]{1,0:T(8,128)(2,1)S(1)}, u32[]{:S(2)}, u32[]{:S(2)}) %collective-permute-start.3) | collective-permute-done | bytes 16416 | tf_op jit(solution)/shard_map/ppermute | solution.py:276
  11.2 0.4 %collective-permute-start.6 = (bf16[64,128]{1,0:T(8,128)(2,1)S(1)}, bf16[64,128]{1,0:T(8,128)(2,1)S(1)}, u32[]{:S(2)}, u32[]{:S(2)}) collective-permute-start(bf16[64,128]{1,0:T(8,128)(2,1)S(1)} %collective-permute-done.3.refs_3_), channel_id=1, source_target_pairs={{0,1},{1,0},{2,3},{3,2},{4,5},{5,4},{6,7},{7,6},{8,9},{9,8},{10,11... | collective-permute-start | bytes 49160 | tf_op jit(solution)/shard_map/ppermute | solution.py:280
  11.6 0.0 collective-permute-done.2.refs_2_
  11.6 0.1 collective-permute-start.5
  11.7 1.4 %collective-permute-done.1.refs_1_ = bf16[64,128]{1,0:T(8,128)(2,1)S(1)} collective-permute-done((bf16[64,128]{1,0:T(8,128)(2,1)S(1)}, bf16[64,128]{1,0:T(8,128)(2,1)S(1)}, u32[]{:S(2)}, u32[]{:S(2)}) %collective-permute-start.1) | collective-permute-done | bytes 16416 | tf_op jit(solution)/shard_map/ppermute | solution.py:276
  13.2 0.0 collective-permute-done.7.refs_7_
  13.2 0.0 collective-permute-done.6.refs_6_
  13.2 0.0 collective-permute-done.5.refs_5_
  13.2 2.2 %solve.1 = f32[8,512]{1,0:T(8,128)} custom-call(bf16[64,128]{1,0:T(8,128)(2,1)S(1)} %sketch.1.refs_0_, bf16[64,128]{1,0:T(8,128)(2,1)S(1)} %collective-permute-done.1.refs_1_, bf16[64,128]{1,0:T(8,128)(2,1)S(1)} %collective-permute-done.2.refs_2_, bf16[64,128]{1,0:T(8,128)(2,1)S(1)} %collective-permute-done.3.refs_3_, ...), custom_call_target="tpu_custom_call" | custom-call | tf_op jit(solution)/shard_map/solve/pallas_call | solution.py:264
Async XLA Ops:
  2.3 1.6 %collective-permute-start = (f32[64,128]{1,0:T(8,128)S(1)}, f32[64,128]{1,0:T(8,128)S(1)}, u32[]{:S(2)}, u32[]{:S(2)}) collective-permute-start(f32[64,128]{1,0:T(8,128)S(1)} %get-tuple-element.8.mine_ref), channel_id=1, source_target_pairs={{0,1},{1,0},{2,3},{3,2},{4,5},{5,4},{6,7},{7,6},{8,9},{9,8},{10,11... | collective-permute-start | bytes 98312 | tf_op jit(solution)/shard_map/ppermute | solution.py:280
  4.1 6.5 %collective-permute-start.4 = (bf16[64,128]{1,0:T(8,128)(2,1)S(1)}, bf16[64,128]{1,0:T(8,128)(2,1)S(1)}, u32[]{:S(2)}, u32[]{:S(2)}) collective-permute-start(bf16[64,128]{1,0:T(8,128)(2,1)S(1)} %sketch.1.refs_0_), channel_id=1, source_target_pairs={{0,7},{1,3},{2,4},{3,14},{4,8},{5,6},{6,10},{7,5},{8,12},{9,11},{1... | collective-permute-start | bytes 49160 | tf_op jit(solution)/shard_map/ppermute | solution.py:276
  7.7 3.5 %collective-permute-start.3 = (bf16[64,128]{1,0:T(8,128)(2,1)S(1)}, bf16[64,128]{1,0:T(8,128)(2,1)S(1)}, u32[]{:S(2)}, u32[]{:S(2)}) collective-permute-start(bf16[64,128]{1,0:T(8,128)(2,1)S(1)} %sketch.1.refs_0_), channel_id=1, source_target_pairs={{0,11},{1,5},{2,10},{3,9},{4,13},{5,15},{6,12},{7,0},{8,2},{9,14},... | collective-permute-start | bytes 49160 | tf_op jit(solution)/shard_map/ppermute | solution.py:276
  7.7 3.9 %collective-permute-start.2 = (bf16[64,128]{1,0:T(8,128)(2,1)S(1)}, bf16[64,128]{1,0:T(8,128)(2,1)S(1)}, u32[]{:S(2)}, u32[]{:S(2)}) collective-permute-start(bf16[64,128]{1,0:T(8,128)(2,1)S(1)} %sketch.1.refs_0_), channel_id=1, source_target_pairs={{0,13},{1,14},{2,7},{3,0},{4,10},{5,3},{6,8},{7,2},{8,5},{9,1},{10... | collective-permute-start | bytes 49160 | tf_op jit(solution)/shard_map/ppermute | solution.py:276
  8.2 5.0 %collective-permute-start.1 = (bf16[64,128]{1,0:T(8,128)(2,1)S(1)}, bf16[64,128]{1,0:T(8,128)(2,1)S(1)}, u32[]{:S(2)}, u32[]{:S(2)}) collective-permute-start(bf16[64,128]{1,0:T(8,128)(2,1)S(1)} %sketch.1.refs_0_), channel_id=1, source_target_pairs={{0,9},{1,8},{2,13},{3,12},{4,1},{5,0},{6,15},{7,14},{8,6},{9,7},{1... | collective-permute-start | bytes 49160 | tf_op jit(solution)/shard_map/ppermute | solution.py:276
  10.6 2.6 %collective-permute-start.7 = (bf16[64,128]{1,0:T(8,128)(2,1)S(1)}, bf16[64,128]{1,0:T(8,128)(2,1)S(1)}, u32[]{:S(2)}, u32[]{:S(2)}) collective-permute-start(bf16[64,128]{1,0:T(8,128)(2,1)S(1)} %collective-permute-done.4.refs_4_), channel_id=1, source_target_pairs={{0,1},{1,0},{2,3},{3,2},{4,5},{5,4},{6,7},{7,6},{8,9},{9,8},{10,11... | collective-permute-start | bytes 49160 | tf_op jit(solution)/shard_map/ppermute | solution.py:280
  11.2 2.0 %collective-permute-start.6 = (bf16[64,128]{1,0:T(8,128)(2,1)S(1)}, bf16[64,128]{1,0:T(8,128)(2,1)S(1)}, u32[]{:S(2)}, u32[]{:S(2)}) collective-permute-start(bf16[64,128]{1,0:T(8,128)(2,1)S(1)} %collective-permute-done.3.refs_3_), channel_id=1, source_target_pairs={{0,1},{1,0},{2,3},{3,2},{4,5},{5,4},{6,7},{7,6},{8,9},{9,8},{10,11... | collective-permute-start | bytes 49160 | tf_op jit(solution)/shard_map/ppermute | solution.py:280
  11.6 1.6 %collective-permute-start.5 = (bf16[64,128]{1,0:T(8,128)(2,1)S(1)}, bf16[64,128]{1,0:T(8,128)(2,1)S(1)}, u32[]{:S(2)}, u32[]{:S(2)}) collective-permute-start(bf16[64,128]{1,0:T(8,128)(2,1)S(1)} %collective-permute-done.2.refs_2_), channel_id=1, source_target_pairs={{0,1},{1,0},{2,3},{3,2},{4,5},{5,4},{6,7},{7,6},{8,9},{9,8},{10,11... | collective-permute-start | bytes 49160 | tf_op jit(solution)/shard_map/ppermute | solution.py:280
